TPU v7x, 32 devices: a whole 2x2x4 slice. The times are simulated.
32 devices in a mesh: fsdp: 16 (over z, y, x), rep: 2 (over core).
Axes of the slice: x: 2, y: 2, z: 4, core: 2. Of those that a mesh axis runs over, the one named last changes fastest.
Arguments:
- hidden_in: bfloat16 [16384, 768], P(('fsdp', 'rep')), may hold values from -6 to 6
- caption_lengths: int32 [32, 16], P(('fsdp', 'rep')), may hold values from 1 to 40, 512 in all within a row
- norm_gain: bfloat16 [2, 2, 768], P(None, None, ('fsdp', 'rep')), may hold values from 0.5 to 1.5
- norm_bias: bfloat16 [2, 2, 768], P(None, None, ('fsdp', 'rep')), may hold values from -3 to 3
- qkv_weight: bfloat16 [2, 768, 2304], P(None, ('fsdp', 'rep')), may hold values from -0.21875 to 0.21875
- out_weight: bfloat16 [2, 768, 768], P(None, ('fsdp', 'rep')), may hold values from -1.25 to 1.25
- up_weight: bfloat16 [2, 768, 3072], P(None, ('fsdp', 'rep')), may hold values from -0.21875 to 0.21875
- up_bias: bfloat16 [2, 3072], P(None, ('fsdp', 'rep')), may hold values from -3 to 3
- down_weight: bfloat16 [2, 3072, 768], P(None, ('fsdp', 'rep')), may hold values from -0.109375 to 0.109375
- down_bias: bfloat16 [2, 768], P(None, ('fsdp', 'rep')), may hold values from -3 to 3
- grad_out: bfloat16 [16384, 768], P(('fsdp', 'rep')), may hold values from -6 to 6
Outputs:
- hidden_out: float32 [16384, 768], P(('fsdp', 'rep'))
- d_hidden_in: float32 [16384, 768], P(('fsdp', 'rep'))
- d_norm_gain: float32 [2, 2, 768], P(None, None, ('fsdp', 'rep'))
- d_norm_bias: float32 [2, 2, 768], P(None, None, ('fsdp', 'rep'))
- d_up_weight: float32 [2, 768, 3072], P(None, ('fsdp', 'rep'))
- d_up_bias: float32 [2, 3072], P(None, ('fsdp', 'rep'))
- d_down_weight: float32 [2, 3072, 768], P(None, ('fsdp', 'rep'))
- d_down_bias: float32 [2, 768], P(None, ('fsdp', 'rep'))
Inputs may be any that keep to these rules, and one draw needn't show every extreme that they name: `caption_lengths`: each row's 16 caption lengths add up to 512.
All inputs are finite; a program needn't handle non-finite values.
Results may differ from a plain program's by a relative error of at most 0.015.
Values may be sent and summed in bfloat16 or wider, within the bound.
A program may use at most 256 MiB of HBM per device.

v0:
```python
import jax
import jax.numpy as jnp
from jax import lax
from jax.sharding import PartitionSpec as P

D = 768
FF = 3072
HEADS = 12
SEQ = 512
LAYERS = 2


EPSILON = 1e-05
SCALE = 0.125


def layer_norm(values, gain, shift):
    centre = jnp.mean(values, axis=-1, keepdims=True)
    centred = values - centre
    spread = jnp.mean(centred * centred, axis=-1, keepdims=True)
    return centred * lax.rsqrt(spread + EPSILON) * gain + shift


def exact_gelu(values):
    return jax.nn.gelu(values, approximate=False)


def caption_ids(lengths):
    starts = jnp.cumsum(lengths, axis=-1) - lengths
    places = jnp.arange(SEQ, dtype=jnp.int32)
    passed = (places[None, :, None] >= starts[:, None, :]).astype(jnp.int32)
    return jnp.sum(passed, axis=-1) - 1


def transposed_left(left, right):
    return lax.dot_general(
        left, right, (((0,), (0,)), ((), ())), preferred_element_type=jnp.float32
    )


def transposed_right(left, right):
    return lax.dot_general(
        left, right, (((1,), (1,)), ((), ())), preferred_element_type=jnp.float32
    )


def split_heads(packed):
    width = D // HEADS
    queries = packed[:, :D].reshape(SEQ, HEADS, width)
    keys_part = packed[:, D : 2 * D].reshape(SEQ, HEADS, width)
    values_part = packed[:, 2 * D :].reshape(SEQ, HEADS, width)
    return (queries, keys_part, values_part)


def masked_scores(queries, keys_part, caption):
    scores = (
        jnp.einsum("qhd,khd->hqk", queries, keys_part, preferred_element_type=jnp.float32) * SCALE
    )
    same = caption[:, None] == caption[None, :]
    return jnp.where(same[None], scores, -1e30)


def attend_row(inputs):
    packed, caption = inputs
    queries, keys_part, values_part = split_heads(packed)
    scores = masked_scores(queries, keys_part, caption)
    highest = jnp.max(scores, axis=-1, keepdims=True)
    weights = jnp.exp(scores - highest)
    totals = jnp.sum(weights, axis=-1, keepdims=True)
    probs = (weights / totals).astype(jnp.bfloat16)
    mixed = jnp.einsum("hqk,khd->qhd", probs, values_part, preferred_element_type=jnp.float32)
    return (mixed.reshape(SEQ, D), highest + jnp.log(totals))


def attend_back(inputs):
    packed, caption, logsum, d_mixed = inputs
    queries, keys_part, values_part = split_heads(packed)
    probs = jnp.exp(masked_scores(queries, keys_part, caption) - logsum)
    d_heads = d_mixed.reshape(SEQ, HEADS, D // HEADS)
    d_values = jnp.einsum(
        "hqk,qhd->khd", probs.astype(jnp.bfloat16), d_heads, preferred_element_type=jnp.float32
    )
    d_probs = jnp.einsum("qhd,khd->hqk", d_heads, values_part, preferred_element_type=jnp.float32)
    centre = jnp.sum(d_probs * probs, axis=-1, keepdims=True)
    d_scores = (probs * (d_probs - centre)).astype(jnp.bfloat16)
    d_queries = (
        jnp.einsum("hqk,khd->qhd", d_scores, keys_part, preferred_element_type=jnp.float32) * SCALE
    )
    d_keys = (
        jnp.einsum("hqk,qhd->khd", d_scores, queries, preferred_element_type=jnp.float32) * SCALE
    )
    joined = jnp.concatenate(
        [d_queries.reshape(SEQ, D), d_keys.reshape(SEQ, D), d_values.reshape(SEQ, D)], axis=1
    )
    return joined.astype(jnp.bfloat16)


def fetch_forward(w_qkv, w_out, w_up, w_down, gains, shifts, b_up, b_down):
    return (
        lax.all_gather(w_qkv, ("fsdp", "rep"), axis=0, tiled=True),
        lax.all_gather(w_out, ("fsdp", "rep"), axis=0, tiled=True),
        lax.all_gather(w_up, ("fsdp", "rep"), axis=0, tiled=True),
        lax.all_gather(w_down, ("fsdp", "rep"), axis=0, tiled=True),
        lax.all_gather(gains, ("fsdp", "rep"), axis=1, tiled=True),
        lax.all_gather(shifts, ("fsdp", "rep"), axis=1, tiled=True),
        lax.all_gather(b_up, ("fsdp", "rep"), axis=0, tiled=True),
        lax.all_gather(b_down, ("fsdp", "rep"), axis=0, tiled=True),
    )


def fetch_backward(w_qkv, w_out, w_up, w_down, gains, shifts):
    return (
        lax.all_gather(w_qkv, ("fsdp", "rep"), axis=0, tiled=True),
        lax.all_gather(w_out, ("fsdp", "rep"), axis=0, tiled=True),
        lax.all_gather(w_up, ("fsdp", "rep"), axis=0, tiled=True),
        lax.all_gather(w_down, ("fsdp", "rep"), axis=0, tiled=True),
        lax.all_gather(gains, ("fsdp", "rep"), axis=1, tiled=True),
        lax.all_gather(shifts, ("fsdp", "rep"), axis=1, tiled=True),
    )


def owner_major(matrix, owners):
    width = matrix.shape[1] // owners
    return matrix.reshape(matrix.shape[0], owners, width).transpose(1, 0, 2).reshape(owners, -1)


def settle(d_up, d_down, d_gains, d_shifts, d_bup, d_bdown):
    owners = lax.axis_size("fsdp") * lax.axis_size("rep")
    members = [
        d_up.reshape(owners, -1),
        d_down.reshape(owners, -1),
        owner_major(d_gains, owners),
        owner_major(d_shifts, owners),
        d_bup.reshape(owners, -1),
        d_bdown.reshape(owners, -1),
    ]
    flat = jnp.concatenate(members, axis=1)
    mine = lax.psum_scatter(flat, ("fsdp", "rep"), scatter_dimension=0, tiled=True)
    mine = mine.reshape(-1)
    up_rows = D // owners
    down_rows = FF // owners
    norm_cols = D // owners
    sizes = [up_rows * FF, down_rows * D, 2 * norm_cols, 2 * norm_cols, down_rows, norm_cols]
    pieces = []
    begin = 0
    for length in sizes:
        pieces.append(mine[begin : begin + length])
        begin = begin + length
    return (
        pieces[0].reshape(up_rows, FF),
        pieces[1].reshape(down_rows, D),
        pieces[2].reshape(2, norm_cols),
        pieces[3].reshape(2, norm_cols),
        pieces[4],
        pieces[5],
    )


def per_device(
    hidden_in,
    caption_lengths,
    norm_gain,
    norm_bias,
    qkv_weight,
    out_weight,
    up_weight,
    up_bias,
    down_weight,
    down_bias,
    grad_out,
):
    row_count = caption_lengths.shape[0]
    captions = caption_ids(caption_lengths)
    hidden = hidden_in.astype(jnp.float32)
    stored = []
    for layer_number in range(LAYERS):
        fetched = fetch_forward(
            qkv_weight[layer_number],
            out_weight[layer_number],
            up_weight[layer_number],
            down_weight[layer_number],
            norm_gain[layer_number],
            norm_bias[layer_number],
            up_bias[layer_number],
            down_bias[layer_number],
        )
        w_qkv, w_out, w_up, w_down, gains, shifts, b_up, b_down = fetched
        gains_full = gains.astype(jnp.float32)
        shifts_full = shifts.astype(jnp.float32)
        normed_a = layer_norm(hidden, gains_full[0], shifts_full[0]).astype(jnp.bfloat16)
        packed = jnp.dot(normed_a, w_qkv, preferred_element_type=jnp.float32).astype(jnp.bfloat16)
        mixed, logsum = lax.map(attend_row, (packed.reshape(row_count, SEQ, 3 * D), captions))
        mixed = mixed.reshape(-1, D).astype(jnp.bfloat16)
        middle = hidden + jnp.dot(mixed, w_out, preferred_element_type=jnp.float32)
        normed_f = layer_norm(middle, gains_full[1], shifts_full[1]).astype(jnp.bfloat16)
        preact = jnp.dot(normed_f, w_up, preferred_element_type=jnp.float32) + b_up.astype(
            jnp.float32
        )
        active = exact_gelu(preact).astype(jnp.bfloat16)
        output = (
            middle
            + jnp.dot(active, w_down, preferred_element_type=jnp.float32)
            + b_down.astype(jnp.float32)
        )
        weights_kept = None
        stored.append((hidden, packed, logsum, middle, normed_f, preact, active, weights_kept))
        hidden = output
    gradient = grad_out.astype(jnp.float32)
    settled = [None] * LAYERS
    for layer_number in reversed(range(LAYERS)):
        layer_in, packed, logsum, middle, normed_f, preact, active, weights_kept = stored[
            layer_number
        ]
        fetched = fetch_backward(
            qkv_weight[layer_number],
            out_weight[layer_number],
            up_weight[layer_number],
            down_weight[layer_number],
            norm_gain[layer_number],
            norm_bias[layer_number],
        )
        w_qkv, w_out, w_up, w_down, gains, shifts = fetched
        gains_full = gains.astype(jnp.float32)
        shifts_full = shifts.astype(jnp.float32)
        grad_low = gradient.astype(jnp.bfloat16)
        d_bdown = jnp.sum(grad_low.astype(jnp.float32), axis=0)
        d_down = transposed_left(active, grad_low)
        d_active = transposed_right(grad_low, w_down)
        gelu_value, gelu_back = jax.vjp(exact_gelu, preact)
        d_preact = gelu_back(d_active)[0].astype(jnp.bfloat16)
        d_bup = jnp.sum(d_preact.astype(jnp.float32), axis=0)
        d_up = transposed_left(normed_f, d_preact)
        d_normed_f = transposed_right(d_preact, w_up)
        norm_value, norm_back = jax.vjp(layer_norm, middle, gains_full[1], shifts_full[1])
        d_middle_ln, d_gain_f, d_shift_f = norm_back(d_normed_f)
        d_middle = gradient + d_middle_ln
        d_mixed = transposed_right(d_middle.astype(jnp.bfloat16), w_out).astype(jnp.bfloat16)
        d_packed = lax.map(
            attend_back,
            (
                packed.reshape(row_count, SEQ, 3 * D),
                captions,
                logsum,
                d_mixed.reshape(row_count, SEQ, D),
            ),
        )
        d_normed_a = transposed_right(d_packed.reshape(-1, 3 * D), w_qkv)
        first_value, first_back = jax.vjp(layer_norm, layer_in, gains_full[0], shifts_full[0])
        d_input_ln, d_gain_a, d_shift_a = first_back(d_normed_a)
        gradient = d_middle + d_input_ln
        settled[layer_number] = settle(
            d_up,
            d_down,
            jnp.stack([d_gain_a, d_gain_f]),
            jnp.stack([d_shift_a, d_shift_f]),
            d_bup,
            d_bdown,
        )
    d_gains = jnp.stack([settled[number][2] for number in range(LAYERS)])
    d_shifts = jnp.stack([settled[number][3] for number in range(LAYERS)])
    d_up_all = jnp.stack([settled[number][0] for number in range(LAYERS)])
    d_bup_all = jnp.stack([settled[number][4] for number in range(LAYERS)])
    d_down_all = jnp.stack([settled[number][1] for number in range(LAYERS)])
    d_bdown_all = jnp.stack([settled[number][5] for number in range(LAYERS)])
    return (hidden, gradient, d_gains, d_shifts, d_up_all, d_bup_all, d_down_all, d_bdown_all)


def solution(mesh):
    in_specs = (
        P(("fsdp", "rep"), None),
        P(("fsdp", "rep"), None),
        P(None, None, ("fsdp", "rep")),
        P(None, None, ("fsdp", "rep")),
        P(None, ("fsdp", "rep"), None),
        P(None, ("fsdp", "rep"), None),
        P(None, ("fsdp", "rep"), None),
        P(None, ("fsdp", "rep")),
        P(None, ("fsdp", "rep"), None),
        P(None, ("fsdp", "rep")),
        P(("fsdp", "rep"), None),
    )
    out_specs = (
        P(("fsdp", "rep"), None),
        P(("fsdp", "rep"), None),
        P(None, None, ("fsdp", "rep")),
        P(None, None, ("fsdp", "rep")),
        P(None, ("fsdp", "rep"), None),
        P(None, ("fsdp", "rep")),
        P(None, ("fsdp", "rep"), None),
        P(None, ("fsdp", "rep")),
    )
    return jax.shard_map(
        per_device, mesh=mesh, in_specs=in_specs, out_specs=out_specs, check_vma=False
    )
```

profile of v0, /device:TPU:0, one launch (start us, length us, event | category | flops | bytes accessed | tf_op | source)
XLA Modules:
  0.0 1286.9 jit_solution(6572016467053034267)
XLA Ops:
  19.1 42.4 %all-reduce.7 = (bf16[3072]{0:T(1024)(128)(2,1)S(1)}, bf16[768]{0:T(1024)(128)(2,1)S(1)}, bf16[3072]{0:T(1024)(128)(2,1)S(1)}, bf16[768]{0:T(1024)(128)(2,1)}) all-reduce(bf16[3072]{0:T(1024)(128)(2,1)S(1)} %dynamic-update-slice, bf16[768]{0:T(1024)(128)(2,1)S(1)} %dynamic-update-slice.1, ...), channel_id=7, replica_groups=mesh['fsdp'=16,'rep'=2] {'fsdp','rep'}, use_global_device_ids=true, to_apply=%add | all-reduce | flops 7680 | bytes 30720
  62.3 42.1 %all-gather.1 = bf16[1,2,768]{1,0,2:T(2,128)(2,1)S(1)} all-gather(bf16[1,2,24]{1,0,2:T(2,128)(2,1)S(1)} %copy.160), channel_id=3, replica_groups=mesh['fsdp'=16,'rep'=2] {'fsdp','rep'}, dimensions={2}, use_global_device_ids=true | all-gather | bytes 3168 | tf_op jit(solution)/shard_map/all_gather | solution.py:105
  110.2 38.0 %all-gather = bf16[1,2,768]{1,0,2:T(2,128)(2,1)S(1)} all-gather(bf16[1,2,24]{1,0,2:T(2,128)(2,1)S(1)} %copy.159), channel_id=2, replica_groups=mesh['fsdp'=16,'rep'=2] {'fsdp','rep'}, dimensions={2}, use_global_device_ids=true | all-gather | bytes 3168 | tf_op jit(solution)/shard_map/all_gather | solution.py:104
  154.8 39.7 %all-gather.9 = bf16[1,2,768]{1,0,2:T(2,128)(2,1)S(1)} all-gather(bf16[1,2,24]{1,0,2:T(2,128)(2,1)S(1)} %copy.162), channel_id=11, replica_groups=mesh['fsdp'=16,'rep'=2] {'fsdp','rep'}, dimensions={2}, use_global_device_ids=true | all-gather | bytes 3168 | tf_op jit(solution)/shard_map/all_gather | solution.py:105
  199.6 38.7 %all-gather.8 = bf16[1,2,768]{1,0,2:T(2,128)(2,1)S(1)} all-gather(bf16[1,2,24]{1,0,2:T(2,128)(2,1)S(1)} %copy.161), channel_id=10, replica_groups=mesh['fsdp'=16,'rep'=2] {'fsdp','rep'}, dimensions={2}, use_global_device_ids=true | all-gather | bytes 3168 | tf_op jit(solution)/shard_map/all_gather | solution.py:104
  265.6 19.8 %multiply_convert_fusion.3 = (bf16[512,3072]{1,0:T(8,128)(2,1)}, f32[512,3072]{1,0:T(8,128)}, f32[512,3072]{1,0:T(8,128)}) fusion(f32[3072]{0:T(1024)S(1)} %convert_element_type.196, bf16[1,768,3072]{2,1,0:T(8,128)(2,1)} %all-gather.29.cloned.1.call-done, f32[512,768]{1,0:T(8,128)S(1)} %get-tuple-element.147, f32[768]{0:T(1024)S(1)} %get-tuple-element.101, ...), kind=kOutput, calls=%fused_computation.41 | convolution fusion | flops 2521694208 | bytes 22042624 | tf_op jit(solution)/shard_map/dot_general | solution.py:196
  285.4 6.4 fusion.137
  292.1 33.5 %all-gather.33.cloned.1.call-done = bf16[1,768,2304]{2,1,0:T(8,128)(2,1)} async-done(((bf16[1,24,2304]{2,1,0:T(8,128)(2,1)}), bf16[1,768,2304]{2,1,0:T(8,128)(2,1)}) %all-gather.33.cloned.1.call-update) | async-done | bytes 3538960 | tf_op jit(solution)/shard_map/all_gather | solution.py:100
  345.4 35.9 %all-gather.35.cloned.1.call-done = bf16[1,768,768]{2,1,0:T(8,128)(2,1)} async-done(((bf16[1,24,768]{2,1,0:T(8,128)(2,1)}), bf16[1,768,768]{2,1,0:T(8,128)(2,1)}) %all-gather.35.cloned.1.call-update) | async-done | bytes 1179664 | tf_op jit(solution)/shard_map/all_gather | solution.py:101
  384.8 62.6 %all-gather.37.cloned.1.call-done = bf16[1,768,3072]{2,1,0:T(8,128)(2,1)} async-done(((bf16[1,24,3072]{2,1,0:T(8,128)(2,1)}), bf16[1,768,3072]{2,1,0:T(8,128)(2,1)}) %all-gather.37.cloned.1.call-update) | async-done | bytes 4718608 | tf_op jit(solution)/shard_map/all_gather | solution.py:102
  447.4 20.1 %multiply_convert_fusion.2 = (bf16[512,3072]{1,0:T(8,128)(2,1)}, f32[512,3072]{1,0:T(8,128)}, f32[512,3072]{1,0:T(8,128)}) fusion(f32[3072]{0:T(1024)} %convert_element_type.198, bf16[1,768,3072]{2,1,0:T(8,128)(2,1)} %all-gather.37.cloned.1.call-done, f32[512,768]{1,0:T(8,128)S(1)} %get-tuple-element.154, f32[768]{0:T(1024)} %get-tuple-element.97, ...), kind=kOutput, calls=%fused_computation.28 | convolution fusion | flops 2521694208 | bytes 22042624 | tf_op jit(solution)/shard_map/dot_general | solution.py:196
  467.5 45.3 %all-gather.39.cloned.1.call-done = bf16[1,3072,768]{2,1,0:T(8,128)(2,1)} async-done(((bf16[1,96,768]{2,1,0:T(8,128)(2,1)}), bf16[1,3072,768]{2,1,0:T(8,128)(2,1)}) %all-gather.39.cloned.1.call-update) | async-done | bytes 4718608 | tf_op jit(solution)/shard_map/all_gather | solution.py:103
  512.8 11.4 convert_reduce_fusion
  530.2 6.5 fusion.77
  536.7 9.6 multiply_reduce_fusion.1
  546.3 7.2 multiply_convert_fusion.1
  561.9 9.5 convert_reduce_fusion.1
  577.4 7.3 fusion.80
  584.8 9.4 multiply_reduce_fusion
  594.3 7.1 multiply_convert_fusion
  605.8 5.5 fusion.121
  611.3 6.1 fusion.120
  625.9 8.1 reshape.459
  634.0 8.0 constant_dynamic-update-slice_fusion.3
  647.0 8.1 reshape.460
  656.0 8.2 reshape.453
  664.1 7.9 constant_dynamic-update-slice_fusion.1
  672.0 8.3 reshape.454
  684.7 8.4 constant_dynamic-update-slice_fusion.2
  713.4 7.3 add_add_fusion.7
  720.7 544.0 %all-reduce.10.cloned.1.call-done = (f32[32,147672]{1,0:T(8,128)}, f32[32,147672]{1,0:T(8,128)}) async-done(((f32[32,147672]{1,0:T(8,128)}, f32[32,147672]{1,0:T(8,128)}), (f32[32,147672]{1,0:T(8,128)}, f32[32,147672]{1,0:T(8,128)})) %all-reduce.10.cloned.1.call-update) | async-done | bytes 37804048
  1268.9 7.1 dynamic-slice_reduce_fusion
  (328 shorter events, 152.6 us)
Async XLA Ops:
  7.2 146.0 %copy-start.4 = (bf16[512,768]{1,0:T(8,128)(2,1)S(1)}, bf16[512,768]{1,0:T(8,128)(2,1)}, u32[]{:S(2)}) copy-start(bf16[512,768]{1,0:T(8,128)(2,1)} %param.11) | copy-start | bytes 2359300
  7.2 146.6 %copy-start.57 = (s32[1,16]{1,0:T(1,128)S(1)}, s32[1,16]{1,0:T(1,128)}, u32[]{:S(2)}) copy-start(s32[1,16]{1,0:T(1,128)} %param.12) | copy-start | bytes 196
  7.2 236.6 %all-gather.25.cloned.1.call-start = ((), (), s32[]{:S(2)}) async-start(), calls=%async_computation | async-start | bytes 3649536 | tf_op jit(solution)/shard_map/all_gather | solution.py:100
  9.0 253.8 %all-gather.27.cloned.1.call-start = ((), (), s32[]{:S(2)}) async-start(), calls=%async_computation.1 | async-start | bytes 1216512 | tf_op jit(solution)/shard_map/all_gather | solution.py:101
  10.5 255.1 %all-gather.29.cloned.1.call-start = ((), (), s32[]{:S(2)}) async-start(), calls=%async_computation.2 | async-start | bytes 4866048 | tf_op jit(solution)/shard_map/all_gather | solution.py:102
  12.3 273.1 %all-gather.31.cloned.1.call-start = ((), (), s32[]{:S(2)}) async-start(), calls=%async_computation.3 | async-start | bytes 4866048 | tf_op jit(solution)/shard_map/all_gather | solution.py:103
  14.1 311.6 %all-gather.33.cloned.1.call-start = ((), (), s32[]{:S(2)}) async-start(), calls=%async_computation.4 | async-start | bytes 3649536 | tf_op jit(solution)/shard_map/all_gather | solution.py:100
  14.7 366.6 %all-gather.35.cloned.1.call-start = ((), (), s32[]{:S(2)}) async-start(), calls=%async_computation.5 | async-start | bytes 1216512 | tf_op jit(solution)/shard_map/all_gather | solution.py:101
  15.2 432.1 %all-gather.37.cloned.1.call-start = ((), (), s32[]{:S(2)}) async-start(), calls=%async_computation.6 | async-start | bytes 4866048 | tf_op jit(solution)/shard_map/all_gather | solution.py:102
  16.0 496.8 %all-gather.39.cloned.1.call-start = ((), (), s32[]{:S(2)}) async-start(), calls=%async_computation.7 | async-start | bytes 4866048 | tf_op jit(solution)/shard_map/all_gather | solution.py:103
  16.7 1247.9 %all-reduce.10.cloned.1.call-start = ((), (), s32[]{:S(2)}) async-start(), calls=%async_computation.8 | async-start | bytes 75628544
  109.4 156.2 %copy-start.49 = (f32[768]{0:T(1024)}, f32[768]{0:T(1024)S(1)}, u32[]{:S(2)}) copy-start(f32[768]{0:T(1024)S(1)} %get-tuple-element.101) | copy-start | bytes 9220
  153.2 90.6 %copy-start.30 = (f32[768]{0:T(1024)}, f32[768]{0:T(1024)S(1)}, u32[]{:S(2)}) copy-start(f32[768]{0:T(1024)S(1)} %get-tuple-element.100) | copy-start | bytes 9220
  153.4 90.4 %copy-start.32 = (f32[512]{0:T(512)}, f32[512]{0:T(512)S(1)}, u32[]{:S(2)}) copy-start(f32[512]{0:T(512)S(1)} %broadcast_multiply_fusion.3) | copy-start | bytes 6148
  153.8 90.0 %copy-start.34 = (f32[512]{0:T(512)}, f32[512]{0:T(512)S(1)}, u32[]{:S(2)}) copy-start(f32[512]{0:T(512)S(1)} %fusion.102) | copy-start | bytes 6148
  265.2 20.2 %copy-start.14 = (f32[512,768]{1,0:T(8,128)}, f32[512,768]{1,0:T(8,128)S(1)}, u32[]{:S(2)}) copy-start(f32[512,768]{1,0:T(8,128)S(1)} %get-tuple-element.147) | copy-start | bytes 4718596
  265.5 19.9 %copy-start.38 = (f32[512]{0:T(512)}, f32[512]{0:T(512)S(1)}, u32[]{:S(2)}) copy-start(f32[512]{0:T(512)S(1)} %multiply_reduce_fusion.10) | copy-start | bytes 6148
  292.1 37.7 %copy-start.46 = (f32[512]{0:T(512)}, f32[512]{0:T(512)S(1)}, u32[]{:S(2)}) copy-start(f32[512]{0:T(512)S(1)} %fusion.104) | copy-start | bytes 6148
  383.7 143.5 %copy-start.2 = (f32[512,768]{1,0:T(8,128)}, f32[512,768]{1,0:T(8,128)S(1)}, u32[]{:S(2)}) copy-start(f32[512,768]{1,0:T(8,128)S(1)} %get-tuple-element.154) | copy-start | bytes 4718596
  447.4 65.4 %copy-start.42 = (f32[3072]{0:T(1024)S(1)}, f32[3072]{0:T(1024)}, u32[]{:S(2)}) copy-start(f32[3072]{0:T(1024)} %convert_element_type.198) | copy-start | bytes 36868
  512.8 11.4 copy-start.45
  512.8 11.4 copy-start.53
  530.2 16.1 %slice-start.3 = ((s8[12582912]{0:T(1024)(128)(4,1)}), s8[4194304]{0:T(1024)(128)(4,1)S(1)}, s32[]{:S(2)}) async-start(s8[12582912]{0:T(1024)(128)(4,1)} %bitcast.158), calls=%async_computation.12 | async-start | bytes 8388608
  530.2 16.1 %slice-start.4 = ((s8[12582912]{0:T(1024)(128)(4,1)}), s8[4194304]{0:T(1024)(128)(4,1)S(1)}, s32[]{:S(2)}) async-start(s8[12582912]{0:T(1024)(128)(4,1)} %bitcast.158), calls=%async_computation.13 | async-start | bytes 8388608
  536.7 9.6 slice-start.5
  560.8 10.6 slice-start.9
  561.8 9.5 copy-start.15
  561.8 9.5 slice-start.10
  575.1 9.7 copy-start.43
  577.4 16.8 %slice-start = ((s8[12582912]{0:T(1024)(128)(4,1)}), s8[4194304]{0:T(1024)(128)(4,1)S(1)}, s32[]{:S(2)}) async-start(s8[12582912]{0:T(1024)(128)(4,1)} %bitcast.156), calls=%async_computation.9 | async-start | bytes 8388608
  577.4 16.8 %slice-start.1 = ((s8[12582912]{0:T(1024)(128)(4,1)}), s8[4194304]{0:T(1024)(128)(4,1)S(1)}, s32[]{:S(2)}) async-start(s8[12582912]{0:T(1024)(128)(4,1)} %bitcast.156), calls=%async_computation.10 | async-start | bytes 8388608
  672.0 11.8 copy-start.41
  (53 other events, 236.5 us)
Sparse Core Ops, SparseCore 0:
  11.5 62.9 all-gather.24
  77.4 53.3 all-gather.26
  134.3 63.9 all-gather.28
  201.6 62.4 all-gather.30
  266.8 58.8 all-gather.32
  328.4 52.8 all-gather.34
  384.8 62.5 all-gather.36
  450.3 62.4 all-gather.38
  709.0 555.6 all-reduce.9
where the time goes:
time: 1290 us
  waiting for transfers between devices  724 us (56%)
  blocking collectives  201 us (16%)
  matrix products  176 us (14%)
  local copies, waits for them, and re-layouts  131 us (10%)
  other arithmetic  39.7 us (3%)
  between operations  15.2 us (1%)
    unnamed x10, waiting for transfers between devices  546 us
    all_gather x2, blocking collectives, fetch_forward(): lax.all_gather(shifts, ('fsdp', 'rep'), axis=1, tiled=True)  81.8 us
    all_gather x2, blocking collectives, fetch_forward(): lax.all_gather(gains, ('fsdp', 'rep'), axis=1, tiled=True)  76.7 us
    all_gather x2, waiting for transfers between devices, fetch_forward(): lax.all_gather(w_up, ('fsdp', 'rep'), axis=0, tiled=True)  62.6 us
    unnamed x176, local copies, waits for them, and re-layouts  47.8 us
    all_gather x2, waiting for transfers between devices, fetch_forward(): lax.all_gather(w_down, ('fsdp', 'rep'), axis=0, tiled=True)  45.3 us
    unnamed x1, blocking collectives  42.4 us
    dot_general x2, matrix products, per_device(): jnp.dot(normed_f, w_up, preferred_element_type=jnp.float32)  39.9 us
  transfers between devices with their start and end apart: 9, of which 5 were waited for; matrix products, arithmetic and copies ran while one was open for 10% of the time, Pallas kernels for 0%

commit v1 on v0

--- a/solution.py
+++ b/solution.py
@@ -2,6 +2,10 @@
 import jax.numpy as jnp
 from jax import lax
 from jax.sharding import PartitionSpec as P
+from jax.experimental import pallas as pl
+from jax.experimental.pallas import tpu as pltpu
+
+MESH = pl.DeviceIdType.MESH
 
 D = 768
 FF = 3072
@@ -95,12 +99,293 @@
     return joined.astype(jnp.bfloat16)
 
 
-def fetch_forward(w_qkv, w_out, w_up, w_down, gains, shifts, b_up, b_down):
+ZS, YS, XS = 4, 2, 2
+
+
+class Place:
+    def __init__(self):
+        f = lax.axis_index("fsdp")
+        c = lax.axis_index("rep")
+        self.f, self.c = f, c
+        self.x = f % 2
+        self.y = (f // 2) % 2
+        self.z = f // 4
+        fx = f + 1 - 2 * self.x
+        fy = f + 2 - 4 * self.y
+        self.fa = fx + c * (fy - fx)
+        self.fb = fy + c * (fx - fy)
+        self.ya = (self.fa // 2) % 2
+        self.xa = self.fa % 2
+        self.yb = (self.fb // 2) % 2
+        self.xb = self.fb % 2
+        self.A = (self.fa, c)
+        self.B = (self.fb, c)
+        self.C = (f, 1 - c)
+        self.UP = (f + 4, c)
+        self.DN = (f - 4, c)
+        self.has_up = self.z < 3
+        self.has_dn = self.z > 0
+        z = self.z
+        self.order = [z]
+        tables = [(0, 1, 2, 3), (1, 0, 2, 3), (2, 1, 3, 0), (3, 2, 1, 0)]
+        for i in range(1, 4):
+            v = jnp.int32(tables[3][i])
+            for zz in (2, 1, 0):
+                v = jnp.where(z == zz, tables[zz][i], v)
+            self.order.append(v)
+
+    def barrier(self):
+        bar = pltpu.get_barrier_semaphore()
+        for d in (self.A, self.B, self.C):
+            pl.semaphore_signal(bar, inc=1, device_id=d, device_id_type=MESH)
+
+        @pl.when(self.has_up)
+        def _():
+            pl.semaphore_signal(bar, inc=1, device_id=self.UP, device_id_type=MESH)
+
+        @pl.when(self.has_dn)
+        def _():
+            pl.semaphore_signal(bar, inc=1, device_id=self.DN, device_id_type=MESH)
+
+        count = 3 + self.has_up.astype(jnp.int32) + self.has_dn.astype(jnp.int32)
+        pl.semaphore_wait(bar, count)
+
+
+class Gather:
+    def __init__(self, place, ref, by_column, k, sems):
+        self.p, self.ref, self.by_column, self.k = place, ref, by_column, k
+        (self.zs, self.as_, self.bs, self.cs, self.zr, self.ar, self.br, self.cr) = sems
+
+    def cut(self, zi, yi, xi, c=None):
+        c = self.p.c if c is None else c
+        if self.by_column:
+            half = self.ref.shape[-1] // 2
+            return self.ref.at[zi, yi, xi, :, pl.ds(pl.multiple_of(c * half, 128), half)]
+        return self.ref.at[zi, yi, xi, c]
+
+    def send(self, piece, to, ssem, rsem):
+        return pltpu.make_async_remote_copy(
+            src_ref=piece, dst_ref=piece, send_sem=ssem, recv_sem=rsem,
+            device_id=to, device_id_type=MESH)
+
+    def wait(self, piece, sem):
+        pltpu.make_async_copy(piece, piece, sem).wait()
+
+    def own(self):
+        p, k = self.p, self.k
+        mine = self.cut(p.z, p.y, p.x)
+
+        @pl.when(p.has_up)
+        def _():
+            self.send(mine, p.UP, self.zs.at[k, 0], self.zr.at[k, p.z]).start()
+
+        @pl.when(p.has_dn)
+        def _():
+            self.send(mine, p.DN, self.zs.at[k, 1], self.zr.at[k, p.z]).start()
+
+        self.send(mine, p.A, self.as_.at[k], self.ar.at[k, p.z]).start()
+        self.send(mine, p.B, self.bs.at[k], self.br.at[k, p.z]).start()
+
+    def forward(self, i):
+        p = self.p
+        zi = p.order[i]
+        up = (zi < p.z) & p.has_up
+        dn = (zi > p.z) & p.has_dn
+        return zi, up, dn
+
+    def zvisit(self, i):
+        p, k = self.p, self.k
+        zi, up, dn = self.forward(i)
+        piece = self.cut(zi, p.y, p.x)
+        self.wait(piece, self.zr.at[k, zi])
+
+        @pl.when(up)
+        def _():
+            self.send(piece, p.UP, self.zs.at[k, 1 + i], self.zr.at[k, zi]).start()
+
+        @pl.when(dn)
+        def _():
+            self.send(piece, p.DN, self.zs.at[k, 1 + i], self.zr.at[k, zi]).start()
+
+        self.send(piece, p.A, self.as_.at[k], self.ar.at[k, zi]).start()
+        self.send(piece, p.B, self.bs.at[k], self.br.at[k, zi]).start()
+
+    def avisit(self, i):
+        p, k = self.p, self.k
+        zi = p.order[i]
+        piece = self.cut(zi, p.ya, p.xa)
+        self.wait(piece, self.ar.at[k, zi])
+        self.send(piece, p.B, self.bs.at[k], self.br.at[k, zi]).start()
+
+    def plane(self, zi, c=None):
+        c = self.p.c if c is None else c
+        if self.by_column:
+            half = self.ref.shape[-1] // 2
+            return self.ref.at[zi, :, :, :, pl.ds(pl.multiple_of(c * half, 128), half)]
+        return self.ref.at[zi, :, :, c]
+
+    def row(self, zi):
+        c = self.p.c
+        if self.by_column:
+            half = self.ref.shape[-1] // 2
+            return self.ref.at[zi, 0, :, :, pl.ds(pl.multiple_of(c * half, 128), half)]
+        return self.ref.at[zi, 0, :, c]
+
+    def bvisit(self, i):
+        p, k = self.p, self.k
+        zi = p.order[i]
+        self.wait(self.row(zi), self.br.at[k, zi])
+        block = self.plane(zi)
+        self.send(block, p.C, self.cs.at[k], self.cr.at[k, zi]).start()
+
+    def cvisit(self, i):
+        p, k = self.p, self.k
+        zi = p.order[i]
+        self.wait(self.plane(zi, 1 - p.c), self.cr.at[k, zi])
+
+    def finish(self):
+        p, k = self.p, self.k
+        one = self.cut(0, 0, 0)
+
+        @pl.when(p.has_up)
+        def _():
+            self.wait(one, self.zs.at[k, 0])
+
+        @pl.when(p.has_dn)
+        def _():
+            self.wait(one, self.zs.at[k, 1])
+
+        for i in range(1, 4):
+            zi, up, dn = self.forward(i)
+
+            @pl.when(up | dn)
+            def _():
+                self.wait(one, self.zs.at[k, 1 + i])
+
+        c = p.c
+        if self.by_column:
+            half = self.ref.shape[-1] // 2
+            cols = pl.ds(pl.multiple_of(c * half, 128), half)
+            self.wait(self.ref.at[:, 0, 0, :, cols], self.as_.at[k])
+            self.wait(self.ref.at[:, 0, :, :, cols], self.bs.at[k])
+            self.wait(self.ref.at[:, :, :, :, cols], self.cs.at[k])
+        else:
+            self.wait(self.ref.at[:, 0, 0, c], self.as_.at[k])
+            self.wait(self.ref.at[:, 0, :, c], self.bs.at[k])
+            self.wait(self.ref.at[:, :, :, c], self.cs.at[k])
+
+
+def gather_sems(n):
+    dma = pltpu.SemaphoreType.DMA
+    return [dma((n, 5)), dma((n,)), dma((n,)), dma((n,)), dma((n, 4)), dma((n, 4)), dma((n, 4)), dma((n, 4))]
+
+
+def pack_rows(qkv, out, up):
+    parts = []
+    for h in range(2):
+        for w in (qkv, out, up):
+            half = w.shape[-1] // 2
+            parts.append(w[:, :, h * half:(h + 1) * half])
+    return jnp.pad(jnp.concatenate(parts, axis=-1), ((0, 0), (0, 8), (0, 0)))
+
+
+WIDTHS = (2304, 768, 3072)
+
+
+def gather_kernel(pin_ref, down_ref, *refs):
+    outs = refs[:8]
+    bufs = refs[8:16]
+    land, psem, osem = refs[16:19]
+    sems = refs[19:]
+    p = Place()
+    p.barrier()
+    c = p.c
+    width = sum(WIDTHS) // 2
+    swaps = []
+    for l in range(LAYERS):
+        cp = pltpu.make_async_remote_copy(
+            src_ref=pin_ref.at[l, :, pl.ds(pl.multiple_of((1 - c) * width, 128), width)],
+            dst_ref=land.at[l], send_sem=psem.at[0, l], recv_sem=psem.at[1, l],
+            device_id=p.C, device_id_type=MESH)
+        cp.start()
+        swaps.append(cp)
+    chunks = []
+    for l in range(LAYERS):
+        for j in range(4):
+            k = l * 4 + j
+            chunks.append(Gather(p, bufs[k], j < 3, k, sems))
+    for l in range(LAYERS):
+        bufs[l * 4 + 3][p.z, p.y, p.x, c] = down_ref[l]
+    for l in range(LAYERS):
+        swaps[l].wait()
+        off = 0
+        for j, n in enumerate(WIDTHS):
+            half = n // 2
+            for cc in range(2):
+                @pl.when(c == cc)
+                def _():
+                    mine = pin_ref[l, 0:24, cc * width + off:cc * width + off + half]
+                    other = land[l, 0:24, off:off + half]
+                    pair = [mine, other] if cc == 0 else [other, mine]
+                    bufs[l * 4 + j][p.z, p.y, p.x, :, cc * half:(cc + 1) * half] = jnp.concatenate(pair, axis=0)
+            off += half
+    n = len(chunks)
+    look = 2
+    for t in range(look):
+        chunks[t].own()
+    for t in range(n + 3):
+        if t + look < n:
+            chunks[t + look].own()
+        if t < n:
+            for i in range(1, 4):
+                chunks[t].zvisit(i)
+        if 0 <= t - 1 < n:
+            for i in range(4):
+                chunks[t - 1].avisit(i)
+        if 0 <= t - 2 < n:
+            for i in range(4):
+                chunks[t - 2].bvisit(i)
+        if 0 <= t - 3 < n:
+            for i in range(4):
+                chunks[t - 3].cvisit(i)
+            pltpu.make_async_copy(bufs[t - 3], outs[t - 3], osem.at[t - 3]).start()
+    for k in range(n):
+        chunks[k].finish()
+        pltpu.make_async_copy(bufs[k], outs[k], osem.at[k]).wait()
+
+
+def gather_all(qkv, out, up, down):
+    pin = pack_rows(qkv, out, up)
+    shapes = []
+    for l in range(LAYERS):
+        for n in WIDTHS:
+            shapes.append((ZS, YS, XS, 48, n))
+        shapes.append((ZS, YS, XS, 2, 96, D))
+    vm = pl.BlockSpec(memory_space=pltpu.VMEM)
+    got = pl.pallas_call(
+        gather_kernel,
+        out_shape=[jax.ShapeDtypeStruct(s, jnp.bfloat16) for s in shapes],
+        in_specs=[vm, vm],
+        out_specs=[pl.BlockSpec(memory_space=pl.ANY)] * 8,
+        scratch_shapes=[pltpu.VMEM(s, jnp.bfloat16) for s in shapes]
+        + [pltpu.VMEM((LAYERS, 32, sum(WIDTHS) // 2), jnp.bfloat16), pltpu.SemaphoreType.DMA((2, 2)), pltpu.SemaphoreType.DMA((8,))]
+        + gather_sems(8),
+        compiler_params=pltpu.CompilerParams(collective_id=0, has_side_effects=True, vmem_limit_bytes=60 * 2**20),
+    )(pin, down)
+    res = []
+    for l in range(LAYERS):
+        res.append([got[l * 4 + j].reshape(D, WIDTHS[j]) for j in range(3)] + [got[l * 4 + 3].reshape(FF, D)])
+    return res
+
+
+def fetch_forward(whole, w_qkv, w_out, w_up, w_down, gains, shifts, b_up, b_down):
+    if whole is None:
+        whole = [
+            lax.all_gather(w, ("fsdp", "rep"), axis=0, tiled=True)
+            for w in (w_qkv, w_out, w_up, w_down)
+        ]
     return (
-        lax.all_gather(w_qkv, ("fsdp", "rep"), axis=0, tiled=True),
-        lax.all_gather(w_out, ("fsdp", "rep"), axis=0, tiled=True),
-        lax.all_gather(w_up, ("fsdp", "rep"), axis=0, tiled=True),
-        lax.all_gather(w_down, ("fsdp", "rep"), axis=0, tiled=True),
+        *whole,
         lax.all_gather(gains, ("fsdp", "rep"), axis=1, tiled=True),
         lax.all_gather(shifts, ("fsdp", "rep"), axis=1, tiled=True),
         lax.all_gather(b_up, ("fsdp", "rep"), axis=0, tiled=True),
@@ -108,12 +393,14 @@
     )
 
 
-def fetch_backward(w_qkv, w_out, w_up, w_down, gains, shifts):
+def fetch_backward(whole, w_qkv, w_out, w_up, w_down, gains, shifts):
+    if whole is None:
+        whole = [
+            lax.all_gather(w, ("fsdp", "rep"), axis=0, tiled=True)
+            for w in (w_qkv, w_out, w_up, w_down)
+        ]
     return (
-        lax.all_gather(w_qkv, ("fsdp", "rep"), axis=0, tiled=True),
-        lax.all_gather(w_out, ("fsdp", "rep"), axis=0, tiled=True),
-        lax.all_gather(w_up, ("fsdp", "rep"), axis=0, tiled=True),
-        lax.all_gather(w_down, ("fsdp", "rep"), axis=0, tiled=True),
+        *whole,
         lax.all_gather(gains, ("fsdp", "rep"), axis=1, tiled=True),
         lax.all_gather(shifts, ("fsdp", "rep"), axis=1, tiled=True),
     )
@@ -170,11 +457,14 @@
     grad_out,
 ):
     row_count = caption_lengths.shape[0]
+    near = lax.axis_size("fsdp") == 16 and lax.axis_size("rep") == 2
+    weights = gather_all(qkv_weight, out_weight, up_weight, down_weight) if near else None
     captions = caption_ids(caption_lengths)
     hidden = hidden_in.astype(jnp.float32)
     stored = []
     for layer_number in range(LAYERS):
         fetched = fetch_forward(
+            weights[layer_number] if near else None,
             qkv_weight[layer_number],
             out_weight[layer_number],
             up_weight[layer_number],
@@ -212,6 +502,7 @@
             layer_number
         ]
         fetched = fetch_backward(
+            weights[layer_number] if near else None,
             qkv_weight[layer_number],
             out_weight[layer_number],
             up_weight[layer_number],

time: 1290 us -> 1240 us (0.961)
  waiting for transfers between devices: 724 us -> 543 us
  Pallas kernels: 0 us -> 128 us
    all_gather x8 -> x0, waiting for transfers between devices: 177 us -> none  [the longest x2 62.6 us: fetch_forward(): lax.all_gather(w_up, ('fsdp', 'rep'), axis=0, tiled=True)]
    pallas_call x0 -> x1, Pallas kernels: none -> 128 us  [gather_all(): pl.pallas_call(gather_kernel, out_shape=[jax.ShapeDtypeStruct(s, jnp.bflo...]
    unnamed x176 -> x193, local copies, waits for them, and re-layouts: 47.8 us -> 53.7 us
    unnamed x10 -> x2, waiting for transfers between devices: 546 us -> 543 us
  transfers between devices with their start and end apart: 9 -> 1, of which waited for: 5 -> 1; matrix products, arithmetic and copies ran while one was open for 10% -> 1% of each run, Pallas kernels for 0% -> 0%
where the time goes in v1:
time: 1240 us; the launch traced here: 1230 us
  waiting for transfers between devices  543 us (44%)
  blocking collectives  201 us (16%)
  matrix products  168 us (14%)
  local copies, waits for them, and re-layouts  134 us (11%)
  Pallas kernels  128 us (10%)
  other arithmetic  37.8 us (3%)
  between operations  15.6 us (1%)
    unnamed x2, waiting for transfers between devices  543 us
    pallas_call x1, Pallas kernels, gather_all(): pl.pallas_call(gather_kernel, out_shape=[jax.ShapeDtypeStruct(s, jnp.bflo...  128 us
    all_gather x2, blocking collectives, fetch_forward(): lax.all_gather(shifts, ('fsdp', 'rep'), axis=1, tiled=True)  83 us
    all_gather x2, blocking collectives, fetch_forward(): lax.all_gather(gains, ('fsdp', 'rep'), axis=1, tiled=True)  75.4 us
    unnamed x193, local copies, waits for them, and re-layouts  53.7 us
    unnamed x1, blocking collectives  42.2 us
    dot_general x2, matrix products, per_device(): jnp.dot(normed_f, w_up, preferred_element_type=jnp.float32)  39.9 us
    dot_general x8, matrix products, transposed_right(): lax.dot_general(left, right, (((1,), (1,)), ((), ())), preferred_element_...  30.5 us
  transfers between devices with their start and end apart: 1, of which 1 were waited for; matrix products, arithmetic and copies ran while one was open for 1% of the time, Pallas kernels for 0%

profile of v1, /device:TPU:0, one launch (start us, length us, event | category | flops | bytes accessed | tf_op | source)
XLA Modules:
  0.0 1227.3 jit_solution(187311928961286826)
XLA Ops:
  9.6 42.2 %all-reduce.8 = (bf16[3072]{0:T(1024)(128)(2,1)S(1)}, bf16[768]{0:T(1024)(128)(2,1)S(1)}, bf16[3072]{0:T(1024)(128)(2,1)S(1)}, bf16[768]{0:T(1024)(128)(2,1)}) all-reduce(bf16[3072]{0:T(1024)(128)(2,1)S(1)} %dynamic-update-slice, bf16[768]{0:T(1024)(128)(2,1)S(1)} %dynamic-update-slice.1, ...), channel_id=4, replica_groups=mesh['fsdp'=16,'rep'=2] {'fsdp','rep'}, use_global_device_ids=true, to_apply=%add.1 | all-reduce | flops 7680 | bytes 30720
  57.8 41.8 %all-gather.1 = bf16[1,2,768]{1,0,2:T(2,128)(2,1)S(1)} all-gather(bf16[1,2,24]{1,0,2:T(2,128)(2,1)S(1)} %copy.160), channel_id=3, replica_groups=mesh['fsdp'=16,'rep'=2] {'fsdp','rep'}, dimensions={2}, use_global_device_ids=true | all-gather | bytes 3168 | tf_op jit(solution)/shard_map/all_gather | solution.py:390
  105.4 37.7 %all-gather = bf16[1,2,768]{1,0,2:T(2,128)(2,1)S(1)} all-gather(bf16[1,2,24]{1,0,2:T(2,128)(2,1)S(1)} %copy.159), channel_id=2, replica_groups=mesh['fsdp'=16,'rep'=2] {'fsdp','rep'}, dimensions={2}, use_global_device_ids=true | all-gather | bytes 3168 | tf_op jit(solution)/shard_map/all_gather | solution.py:389
  150.8 127.7 %shard_map.170 = (bf16[4,2,2,48,2304]{4,3,2,1,0:T(8,128)(2,1)}, bf16[4,2,2,48,768]{4,3,2,1,0:T(8,128)(2,1)}, bf16[4,2,2,48,3072]{4,3,2,1,0:T(8,128)(2,1)}, bf16[...) custom-call(bf16[2,32,6144]{2,1,0:T(8,128)(2,1)} %pad.4.pin_ref, ...), custom_call_target="tpu_custom_call" | custom-call | tf_op jit(solution)/shard_map/pallas_call | solution.py:365
  298.4 41.2 %all-gather.5 = bf16[1,2,768]{1,0,2:T(2,128)(2,1)S(1)} all-gather(bf16[1,2,24]{1,0,2:T(2,128)(2,1)S(1)} %copy.162), channel_id=7, replica_groups=mesh['fsdp'=16,'rep'=2] {'fsdp','rep'}, dimensions={2}, use_global_device_ids=true | all-gather | bytes 3168 | tf_op jit(solution)/shard_map/all_gather | solution.py:390
  344.7 37.7 %all-gather.4 = bf16[1,2,768]{1,0,2:T(2,128)(2,1)S(1)} all-gather(bf16[1,2,24]{1,0,2:T(2,128)(2,1)S(1)} %copy.161), channel_id=6, replica_groups=mesh['fsdp'=16,'rep'=2] {'fsdp','rep'}, dimensions={2}, use_global_device_ids=true | all-gather | bytes 3168 | tf_op jit(solution)/shard_map/all_gather | solution.py:389
  387.4 19.6 %multiply_convert_fusion.3 = (bf16[512,3072]{1,0:T(8,128)(2,1)S(1)}, f32[512,3072]{1,0:T(8,128)}, f32[512,3072]{1,0:T(8,128)}) fusion(f32[3072]{0:T(1024)S(1)} %convert_element_type.198, bf16[768,3072]{1,0:T(8,128)(2,1)} %bitcast.166, f32[512,768]{1,0:T(8,128)S(1)} %get-tuple-element.155, f32[768]{0:T(1024)S(1)} %get-tuple-element.117, ...), kind=kOutput, calls=%fused_computation.49 | convolution fusion | flops 2521694208 | bytes 22042624 | tf_op jit(solution)/shard_map/dot_general | solution.py:486
  407.1 6.2 fusion.113
  426.2 5.2 fusion.62
  432.8 20.3 %multiply_convert_fusion.2 = (bf16[512,3072]{1,0:T(8,128)(2,1)}, f32[512,3072]{1,0:T(8,128)S(1)}, f32[512,3072]{1,0:T(8,128)}) fusion(f32[3072]{0:T(1024)S(1)} %convert_element_type.200, bf16[768,3072]{1,0:T(8,128)(2,1)} %bitcast.172, f32[512,768]{1,0:T(8,128)S(1)} %get-tuple-element.162, f32[768]{0:T(1024)S(1)} %get-tuple-element.113, ...), kind=kOutput, calls=%fused_computation.36 | convolution fusion | flops 2521694208 | bytes 22042624 | tf_op jit(solution)/shard_map/dot_general | solution.py:486
  453.1 6.8 convert_reduce_fusion
  468.8 8.9 fusion.56
  477.8 9.7 multiply_reduce_fusion.1
  487.4 7.2 multiply_convert_fusion.1
  503.2 9.3 convert_reduce_fusion.1
  518.6 7.8 fusion.59
  526.4 9.4 multiply_reduce_fusion
  535.9 7.1 multiply_convert_fusion
  547.3 5.5 fusion.100
  552.9 5.7 fusion.98
  558.6 5.3 fusion.83
  567.3 8.1 reshape.491
  575.3 8.0 constant_dynamic-update-slice_fusion.3
  583.3 5.1 fusion.115
  588.4 8.1 reshape.492
  597.3 8.2 reshape.485
  605.5 7.9 constant_dynamic-update-slice_fusion.1
  613.4 8.2 reshape.486
  625.9 8.4 constant_dynamic-update-slice_fusion.2
  654.8 6.7 add_add_fusion.7
  661.4 543.3 %all-reduce.11.cloned.1.call-done = (f32[32,147672]{1,0:T(8,128)}, f32[32,147672]{1,0:T(8,128)}) async-done(((f32[32,147672]{1,0:T(8,128)}, f32[32,147672]{1,0:T(8,128)}), (f32[32,147672]{1,0:T(8,128)}, f32[32,147672]{1,0:T(8,128)})) %all-reduce.11.cloned.1.call-update) | async-done | bytes 37804048
  1208.9 7.1 dynamic-slice_reduce_fusion
  (322 shorter events, 130.6 us)
Async XLA Ops:
  7.2 142.3 %copy-start.4 = (bf16[512,768]{1,0:T(8,128)(2,1)S(1)}, bf16[512,768]{1,0:T(8,128)(2,1)}, u32[]{:S(2)}) copy-start(bf16[512,768]{1,0:T(8,128)(2,1)} %param.11) | copy-start | bytes 2359300
  7.2 1197.5 %all-reduce.11.cloned.1.call-start = ((), (), s32[]{:S(2)}) async-start(), calls=%async_computation | async-start | bytes 75628544
  104.6 282.7 %copy-start.50 = (f32[768]{0:T(1024)}, f32[768]{0:T(1024)S(1)}, u32[]{:S(2)}) copy-start(f32[768]{0:T(1024)S(1)} %get-tuple-element.117) | copy-start | bytes 9220
  148.1 134.6 %copy-start.30 = (f32[768]{0:T(1024)}, f32[768]{0:T(1024)S(1)}, u32[]{:S(2)}) copy-start(f32[768]{0:T(1024)S(1)} %get-tuple-element.116) | copy-start | bytes 9220
  148.1 239.3 %copy-start.42 = (f32[768]{0:T(1024)}, f32[768]{0:T(1024)S(1)}, u32[]{:S(2)}) copy-start(f32[768]{0:T(1024)S(1)} %get-tuple-element.115) | copy-start | bytes 9220
  149.4 133.3 %copy-start.32 = (f32[512]{0:T(512)}, f32[512]{0:T(512)S(1)}, u32[]{:S(2)}) copy-start(f32[512]{0:T(512)S(1)} %broadcast_multiply_fusion.3) | copy-start | bytes 6148
  149.8 132.9 %copy-start.38 = (f32[512]{0:T(512)}, f32[512]{0:T(512)S(1)}, u32[]{:S(2)}) copy-start(f32[512]{0:T(512)S(1)} %fusion.54) | copy-start | bytes 6148
  149.8 132.9 %copy-start.34 = (f32[512]{0:T(512)}, f32[512]{0:T(512)S(1)}, u32[]{:S(2)}) copy-start(f32[512]{0:T(512)S(1)} %fusion.77) | copy-start | bytes 6148
  298.0 109.1 %copy-start.10 = (f32[512,768]{1,0:T(8,128)}, f32[512,768]{1,0:T(8,128)S(1)}, u32[]{:S(2)}) copy-start(f32[512,768]{1,0:T(8,128)S(1)} %get-tuple-element.155) | copy-start | bytes 4718596
  298.0 109.0 %copy-start.36 = (f32[512]{0:T(512)}, f32[512]{0:T(512)S(1)}, u32[]{:S(2)}) copy-start(f32[512]{0:T(512)S(1)} %broadcast_multiply_fusion.2) | copy-start | bytes 6148
  298.3 108.7 %copy-start.40 = (f32[512]{0:T(512)}, f32[512]{0:T(512)S(1)}, u32[]{:S(2)}) copy-start(f32[512]{0:T(512)S(1)} %multiply_reduce_fusion.10) | copy-start | bytes 6148
  298.3 108.7 %copy-start.45 = (f32[512]{0:T(512)}, f32[512]{0:T(512)S(1)}, u32[]{:S(2)}) copy-start(f32[512]{0:T(512)S(1)} %fusion.78) | copy-start | bytes 6148
  431.5 21.6 %slice-start.9 = ((s8[4718592]{0:T(1024)(128)(4,1)}), s8[4194304]{0:T(1024)(128)(4,1)S(1)}, s32[]{:S(2)}) async-start(s8[4718592]{0:T(1024)(128)(4,1)} %bitcast.163), calls=%async_computation.10 | async-start | bytes 8388608
  431.5 28.4 %slice-start.13 = ((s8[4718592]{0:T(1024)(128)(4,1)}), s8[4194304]{0:T(1024)(128)(4,1)S(1)}, s32[]{:S(2)}) async-start(s8[4718592]{0:T(1024)(128)(4,1)} %bitcast.173), calls=%async_computation.14 | async-start | bytes 8388608
  432.4 30.5 %copy-start.2 = (f32[512,768]{1,0:T(8,128)}, f32[512,768]{1,0:T(8,128)S(1)}, u32[]{:S(2)}) copy-start(f32[512,768]{1,0:T(8,128)S(1)} %get-tuple-element.162) | copy-start | bytes 4718596
  432.7 20.4 %copy-start.23 = (bf16[512,768]{1,0:T(8,128)(2,1)S(1)}, bf16[512,768]{1,0:T(8,128)(2,1)}, u32[]{:S(2)}) copy-start(bf16[512,768]{1,0:T(8,128)(2,1)} %param.21) | copy-start | bytes 2359300
  432.7 20.3 %slice-start.10 = ((s8[4718592]{0:T(1024)(128)(4,1)}), s8[524288]{0:T(1024)(128)(4,1)S(1)}, s32[]{:S(2)}) async-start(s8[4718592]{0:T(1024)(128)(4,1)} %bitcast.163), calls=%async_computation.11 | async-start | bytes 1048576
  432.8 27.1 %slice-start.14 = ((s8[4718592]{0:T(1024)(128)(4,1)}), s8[524288]{0:T(1024)(128)(4,1)S(1)}, s32[]{:S(2)}) async-start(s8[4718592]{0:T(1024)(128)(4,1)} %bitcast.173), calls=%async_computation.15 | async-start | bytes 1048576
  468.8 18.6 %slice-start.3 = ((s8[12582912]{0:T(1024)(128)(4,1)}), s8[4194304]{0:T(1024)(128)(4,1)S(1)}, s32[]{:S(2)}) async-start(s8[12582912]{0:T(1024)(128)(4,1)} %bitcast.131), calls=%async_computation.4 | async-start | bytes 8388608
  468.8 18.6 %slice-start.4 = ((s8[12582912]{0:T(1024)(128)(4,1)}), s8[4194304]{0:T(1024)(128)(4,1)S(1)}, s32[]{:S(2)}) async-start(s8[12582912]{0:T(1024)(128)(4,1)} %bitcast.131), calls=%async_computation.5 | async-start | bytes 8388608
  477.8 9.7 slice-start.5
  502.1 10.4 slice-start.11
  503.1 9.3 copy-start.11
  503.1 9.3 copy-start.37
  503.1 9.3 copy-start.43
  503.1 9.3 copy-start.46
  503.1 9.4 slice-start.12
  516.2 10.2 copy-start.47
  518.6 17.3 %slice-start = ((s8[12582912]{0:T(1024)(128)(4,1)}), s8[4194304]{0:T(1024)(128)(4,1)S(1)}, s32[]{:S(2)}) async-start(s8[12582912]{0:T(1024)(128)(4,1)} %bitcast.129), calls=%async_computation.1 | async-start | bytes 8388608
  518.6 17.3 %slice-start.1 = ((s8[12582912]{0:T(1024)(128)(4,1)}), s8[4194304]{0:T(1024)(128)(4,1)S(1)}, s32[]{:S(2)}) async-start(s8[12582912]{0:T(1024)(128)(4,1)} %bitcast.129), calls=%async_computation.2 | async-start | bytes 8388608
  526.4 9.5 slice-start.2
  613.4 11.6 copy-start.44
  (51 other events, 231.7 us)
Sparse Core Ops, SparseCore 0:
  650.4 554.2 all-reduce.10

commit v2 on v1

--- a/solution.py
+++ b/solution.py
@@ -292,11 +292,11 @@
 WIDTHS = (2304, 768, 3072)
 
 
-def gather_kernel(pin_ref, down_ref, *refs):
-    outs = refs[:8]
-    bufs = refs[8:16]
-    land, psem, osem = refs[16:19]
-    sems = refs[19:]
+def gather_kernel(pin_ref, down_ref, small_ref, *refs):
+    outs = refs[:9]
+    bufs = refs[9:18]
+    land, psem, osem = refs[18:21]
+    sems = refs[21:]
     p = Place()
     p.barrier()
     c = p.c
@@ -314,6 +314,8 @@
         for j in range(4):
             k = l * 4 + j
             chunks.append(Gather(p, bufs[k], j < 3, k, sems))
+    chunks.append(Gather(p, bufs[8], False, 8, sems))
+    bufs[8][p.z, p.y, p.x, c] = small_ref[...]
     for l in range(LAYERS):
         bufs[l * 4 + 3][p.z, p.y, p.x, c] = down_ref[l]
     for l in range(LAYERS):
@@ -354,38 +356,323 @@
         pltpu.make_async_copy(bufs[k], outs[k], osem.at[k]).wait()
 
 
-def gather_all(qkv, out, up, down):
+def gather_all(qkv, out, up, down, small):
     pin = pack_rows(qkv, out, up)
     shapes = []
     for l in range(LAYERS):
         for n in WIDTHS:
             shapes.append((ZS, YS, XS, 48, n))
         shapes.append((ZS, YS, XS, 2, 96, D))
+    shapes.append((ZS, YS, XS, 2, 16, 128))
     vm = pl.BlockSpec(memory_space=pltpu.VMEM)
     got = pl.pallas_call(
         gather_kernel,
         out_shape=[jax.ShapeDtypeStruct(s, jnp.bfloat16) for s in shapes],
-        in_specs=[vm, vm],
-        out_specs=[pl.BlockSpec(memory_space=pl.ANY)] * 8,
+        in_specs=[vm, vm, vm],
+        out_specs=[pl.BlockSpec(memory_space=pl.ANY)] * 9,
         scratch_shapes=[pltpu.VMEM(s, jnp.bfloat16) for s in shapes]
-        + [pltpu.VMEM((LAYERS, 32, sum(WIDTHS) // 2), jnp.bfloat16), pltpu.SemaphoreType.DMA((2, 2)), pltpu.SemaphoreType.DMA((8,))]
-        + gather_sems(8),
+        + [pltpu.VMEM((LAYERS, 32, sum(WIDTHS) // 2), jnp.bfloat16), pltpu.SemaphoreType.DMA((2, 2)), pltpu.SemaphoreType.DMA((9,))]
+        + gather_sems(9),
         compiler_params=pltpu.CompilerParams(collective_id=0, has_side_effects=True, vmem_limit_bytes=60 * 2**20),
-    )(pin, down)
+    )(pin, down, small)
     res = []
     for l in range(LAYERS):
         res.append([got[l * 4 + j].reshape(D, WIDTHS[j]) for j in range(3)] + [got[l * 4 + 3].reshape(FF, D)])
-    return res
-
-
-def fetch_forward(whole, w_qkv, w_out, w_up, w_down, gains, shifts, b_up, b_down):
-    if whole is None:
-        whole = [
-            lax.all_gather(w, ("fsdp", "rep"), axis=0, tiled=True)
-            for w in (w_qkv, w_out, w_up, w_down)
-        ]
+    return res, got[8].reshape(32, 16, 128)
+
+
+class Scatter:
+    def __init__(self, place, k, grad, total, pass_a, pass_z, from_b, from_a, from_dn, from_up, sems):
+        self.p, self.k = place, k
+        self.grad, self.total, self.pass_a, self.pass_z = grad, total, pass_a, pass_z
+        self.from_b, self.from_a, self.from_dn, self.from_up = from_b, from_a, from_dn, from_up
+        self.sb, self.sa, self.sz, self.rb, self.ra, self.rdn, self.rup = sems
+
+    def send(self, src, dst, to, ssem, rsem):
+        pltpu.make_async_remote_copy(
+            src_ref=src, dst_ref=dst, send_sem=ssem, recv_sem=rsem, device_id=to, device_id_type=MESH).start()
+
+    def wait(self, piece, sem):
+        pltpu.make_async_copy(piece, piece, sem).wait()
+
+    def bsend(self, zi):
+        p, k = self.p, self.k
+        self.send(self.grad.at[zi, p.yb, p.xb], self.from_b.at[zi, 0], p.B, self.sb.at[k], self.rb.at[k, zi])
+        self.send(self.grad.at[zi, 1 - p.y, 1 - p.x], self.from_b.at[zi, 1], p.B, self.sb.at[k], self.rb.at[k, zi])
+
+    def bwait(self, zi):
+        p, k = self.p, self.k
+        self.wait(self.from_b.at[zi], self.rb.at[k, zi])
+        part = self.grad[zi, p.ya, p.xa].astype(jnp.float32) + self.from_b[zi, 1].astype(jnp.float32)
+        self.pass_a[zi] = part.astype(self.pass_a.dtype)
+        self.send(self.pass_a.at[zi], self.from_a.at[zi], p.A, self.sa.at[k], self.ra.at[k, zi])
+
+    def await_(self, zi):
+        p, k = self.p, self.k
+        self.wait(self.from_a.at[zi], self.ra.at[k, zi])
+        self.total[zi] = (self.grad[zi, p.y, p.x].astype(jnp.float32)
+                          + self.from_b[zi, 0].astype(jnp.float32)
+                          + self.from_a[zi].astype(jnp.float32))
+
+    def zstep(self, tau):
+        p, k = self.p, self.k
+        z = p.z
+
+        @pl.when((z <= tau) & (z < 3))
+        def _():
+            d = 3 - tau + z
+
+            @pl.when(z > 0)
+            def _():
+                self.wait(self.from_dn.at[d], self.rdn.at[k, d])
+                self.pass_z[d] = (self.total[d] + self.from_dn[d].astype(jnp.float32)).astype(self.pass_z.dtype)
+
+            @pl.when(z == 0)
+            def _():
+                self.pass_z[d] = self.total[d].astype(self.pass_z.dtype)
+
+            self.send(self.pass_z.at[d], self.from_dn.at[d], p.UP, self.sz.at[k], self.rdn.at[k, d])
+
+        @pl.when((3 - z <= tau) & (z > 0))
+        def _():
+            d = tau - 3 + z
+
+            @pl.when(z < 3)
+            def _():
+                self.wait(self.from_up.at[d], self.rup.at[k, d])
+                self.pass_z[d] = (self.total[d] + self.from_up[d].astype(jnp.float32)).astype(self.pass_z.dtype)
+
+            @pl.when(z == 3)
+            def _():
+                self.pass_z[d] = self.total[d].astype(self.pass_z.dtype)
+
+            self.send(self.pass_z.at[d], self.from_up.at[d], p.DN, self.sz.at[k], self.rup.at[k, d])
+
+    def last(self):
+        p, k = self.p, self.k
+        z = p.z
+
+        @pl.when(z > 0)
+        def _():
+            self.wait(self.from_dn.at[z], self.rdn.at[k, z])
+            self.total[z] = self.total[z] + self.from_dn[z].astype(jnp.float32)
+
+        @pl.when(z < 3)
+        def _():
+            self.wait(self.from_up.at[z], self.rup.at[k, z])
+            self.total[z] = self.total[z] + self.from_up[z].astype(jnp.float32)
+
+    def sent_b(self):
+        self.wait(self.from_b, self.sb.at[self.k])
+
+    def sent_a(self):
+        self.wait(self.from_a, self.sa.at[self.k])
+
+    def sent_z(self):
+        self.wait(self.pass_z.at[pl.ds(0, 3)], self.sz.at[self.k])
+
+    def sent(self):
+        self.sent_b()
+        self.sent_a()
+        self.sent_z()
+
+
+def scatter_sems(n):
+    dma = pltpu.SemaphoreType.DMA
+    return [dma((n,)), dma((n,)), dma((n,)), dma((n, 4)), dma((n, 4)), dma((n, 4)), dma((n, 4))]
+
+
+def landing(shard, dtype):
+    return [pltpu.VMEM(s + shard, dtype) for s in ((4, 2), (4,), (4,), (4,))]
+
+
+def passing(shard, dtype):
+    return [pltpu.VMEM((4, 2, 2) + shard, dtype), pltpu.VMEM((4,) + shard, jnp.float32),
+            pltpu.VMEM((4,) + shard, dtype), pltpu.VMEM((4,) + shard, dtype)]
+
+
+LAGS = (2, 4)
+PLANES = (3, 0, 2, 1)
+UP_SHARD = (48, FF // 2)
+DOWN_SHARD = (192, D // 2)
+SMALL_SHARD = (16, 128)
+
+
+def transposed_dot(left, right):
+    return lax.dot_general(left, right, (((0,), (0,)), ((), ())), preferred_element_type=jnp.float32)
+
+
+def scatter_kernel(act_ref, g_ref, nf_ref, dp_ref, small_ref, up_out, down_out, small_out, *refs):
+    land = [refs[4 * k:4 * k + 4] for k in range(5)]
+    up_pass, down_pass = refs[20:24], refs[24:28]
+    small_pass = refs[28:32]
+    act_in, g_in, nf_in, dp_in, small_in, swap = refs[32:38]
+    sems = refs[38:]
+    p = Place()
+    p.barrier()
+    c = p.c
+
+    def remote(src, dst, s, r):
+        return pltpu.make_async_remote_copy(src_ref=src, dst_ref=dst, send_sem=swap.at[0, s], recv_sem=swap.at[1, r], device_id=p.C, device_id_type=MESH)
+
+    mine_g = pl.ds(pl.multiple_of(c * (D // 2), 128), D // 2)
+    mine_dp = pl.ds(pl.multiple_of(c * (FF // 2), 128), FF // 2)
+    other_g = pl.ds(pl.multiple_of((1 - c) * (D // 2), 128), D // 2)
+    other_dp = pl.ds(pl.multiple_of((1 - c) * (FF // 2), 128), FF // 2)
+    swaps = []
+    for l in (1, 0):
+        for i, (src, dst) in enumerate([(act_ref.at[l], act_in.at[l]), (g_ref.at[l, :, other_g], g_in.at[l]),
+                         (nf_ref.at[l], nf_in.at[l]), (dp_ref.at[l, :, other_dp], dp_in.at[l])]):
+            cp = remote(src, dst, l * 4 + i, l * 4 + i)
+            cp.start()
+            swaps.append(cp)
+    cps = remote(small_ref.at[1 - c], small_in, 8, 8)
+    cps.start()
+
+    chunks = []
+    for k in range(4):
+        ps = down_pass if k % 2 == 0 else up_pass
+        chunks.append(Scatter(p, k, *ps, *land[k], sems))
+    small = Scatter(p, 4, *small_pass, *land[4], sems)
+
+    def down_block(l, k, zi):
+        for yi in range(2):
+            cols = pl.ds(768 * zi + 384 * yi, 384)
+            acc = transposed_dot(act_ref[l, :, cols], g_ref[l, :, mine_g]) + transposed_dot(act_in[l, :, cols], g_in[l])
+            chunks[k].grad[zi, yi] = acc.astype(jnp.bfloat16).reshape(2, 192, 384)
+
+    def up_block(l, k, zi):
+        rows = pl.ds(192 * zi, 192)
+        for t in range(3):
+            cols = pl.ds(pl.multiple_of(c * (FF // 2) + 512 * t, 128), 512)
+            acc = transposed_dot(nf_ref[l, :, rows], dp_ref[l, :, cols]) + transposed_dot(nf_in[l, :, rows], dp_in[l, :, pl.ds(512 * t, 512)])
+            chunks[k].grad[zi, :, :, :, pl.ds(512 * t, 512)] = acc.astype(jnp.bfloat16).reshape(2, 2, 48, 512)
+
+    def deliver(k, l):
+        s = chunks[k]
+        s.last()
+        out, rows, half = (down_out, 96, D // 2) if k % 2 == 0 else (up_out, 24, FF // 2)
+        for cc in range(2):
+            @pl.when(c == cc)
+            def _():
+                remote(s.total.at[p.z, pl.ds(rows * (1 - cc), rows)], out.at[l, :, pl.ds(half * cc, half)], 9 + k, 9 + k).start()
+                out[l, :, half * cc:half * (cc + 1)] = s.total[p.z, rows * cc:rows * (cc + 1)]
+
+    def delivered(k, l):
+        out, rows, half = (down_out, 96, D // 2) if k % 2 == 0 else (up_out, 24, FF // 2)
+        cp = remote(chunks[k].total.at[0, pl.ds(0, rows)], out.at[l, :, pl.ds(0, half)], 9 + k, 9 + k)
+        cp.wait_send()
+        cp.wait_recv()
+
+    cps.wait()
+    small.grad[...] = (small_ref[c] + small_in[...])
+    for zi in PLANES:
+        small.bsend(zi)
+    steps = [(k, zi) for k in range(4) for zi in PLANES]
+    n = len(steps)
+    LB, LA = LAGS
+    LZ = LA + 2
+    for t in range(n + LZ + 4):
+        if t < n:
+            k, zi = steps[t]
+            l = 1 - k // 2
+            if t % 4 == 0:
+                for cp in (swaps[0:2] if k % 2 == 0 else swaps[2:4]) if l == 1 else (swaps[4:6] if k % 2 == 0 else swaps[6:8]):
+                    cp.wait()
+                if k >= 2:
+                    chunks[k - 2].sent_b()
+            (down_block if k % 2 == 0 else up_block)(l, k, zi)
+            chunks[k].bsend(zi)
+        if 0 <= t - LB < n:
+            k, zi = steps[t - LB]
+            if (t - LB) % 4 == 0 and k >= 2:
+                chunks[k - 2].sent_a()
+            chunks[k].bwait(zi)
+        if 0 <= t - LA < n:
+            k, zi = steps[t - LA]
+            if (t - LA) % 4 == 0 and k >= 2:
+                chunks[k - 2].sent_z()
+                delivered(k - 2, 1 - (k - 2) // 2)
+            chunks[k].await_(zi)
+        kk = (t - LZ) // 4
+        if t >= LZ and kk < 4:
+            j = (t - LZ) % 4
+            if j < 3:
+                chunks[kk].zstep(j)
+            else:
+                deliver(kk, 1 - kk // 2)
+        if t == 2:
+            for zi in PLANES:
+                small.bwait(zi)
+        if t == 3:
+            for zi in PLANES:
+                small.await_(zi)
+        if 4 <= t < 7:
+            small.zstep(t - 4)
+        if t == 7:
+            small.last()
+            small_out[...] = small.total[p.z]
+    for k in (2, 3):
+        chunks[k].sent()
+        delivered(k, 1 - k // 2)
+    small.sent()
+
+
+def scatter_all(act, g, nf, dp, small):
+    vm = pl.BlockSpec(memory_space=pltpu.VMEM)
+    t = act.shape[1]
+    bf, f32 = jnp.bfloat16, jnp.float32
+    scratch = []
+    for k in range(4):
+        scratch += landing(DOWN_SHARD if k % 2 == 0 else UP_SHARD, bf)
+    scratch += landing(SMALL_SHARD, f32)
+    scratch += passing(UP_SHARD, bf) + passing(DOWN_SHARD, bf) + passing(SMALL_SHARD, f32)
+    scratch += [pltpu.VMEM((2, t, FF), bf), pltpu.VMEM((2, t, D // 2), bf), pltpu.VMEM((2, t, D), bf), pltpu.VMEM((2, t, FF // 2), bf),
+                pltpu.VMEM((4, 2, 2) + SMALL_SHARD, f32), pltpu.SemaphoreType.DMA((2, 16))]
+    scratch += scatter_sems(5)
+    return pl.pallas_call(
+        scatter_kernel,
+        out_shape=[jax.ShapeDtypeStruct((2, 24, FF), f32), jax.ShapeDtypeStruct((2, 96, D), f32), jax.ShapeDtypeStruct(SMALL_SHARD, f32)],
+        in_specs=[vm] * 5,
+        out_specs=[vm] * 3,
+        scratch_shapes=scratch,
+        compiler_params=pltpu.CompilerParams(collective_id=1, has_side_effects=True, vmem_limit_bytes=64000 * 1024),
+    )(act, g, nf, dp, small)
+
+
+def pack_small(gains, shifts, b_up, b_down):
+    wide = lambda v: jnp.pad(v, ((0, 0), (0, 0), (0, 128 - v.shape[-1])))
+    rows = [wide(gains), wide(shifts), wide(b_down[:, None]), wide(b_up[:, None])]
+    rows.append(jnp.zeros((LAYERS, 2, 128), gains.dtype))
+    return jnp.concatenate(rows, axis=1).reshape(16, 128)
+
+
+def unpack_small(whole):
+    whole = whole.reshape(32, LAYERS, 8, 128)
+    per = []
+    for l in range(LAYERS):
+        gains = whole[:, l, 0:2, :24].transpose(1, 0, 2).reshape(2, D)
+        shifts = whole[:, l, 2:4, :24].transpose(1, 0, 2).reshape(2, D)
+        per.append((gains, shifts, whole[:, l, 5, :96].reshape(FF), whole[:, l, 4, :24].reshape(D)))
+    return per
+
+
+def pack_sums(per):
+    layers = []
+    for gains, shifts, b_up, b_down in per:
+        wide = lambda v, n: jnp.pad(v.reshape(-1, 32, n).transpose(1, 0, 2), ((0, 0), (0, 0), (0, 128 - n)))
+        rows = [wide(gains, 24), wide(shifts, 24), wide(b_down, 24), wide(b_up, 96), jnp.zeros((32, 2, 128), jnp.float32)]
+        layers.append(jnp.concatenate(rows, axis=1))
+    both = jnp.concatenate(layers, axis=1)
+    return both.reshape(ZS, YS, XS, 2, 16, 128).transpose(3, 0, 1, 2, 4, 5)
+
+
+def fetch_forward(w_qkv, w_out, w_up, w_down, gains, shifts, b_up, b_down):
     return (
-        *whole,
+        lax.all_gather(w_qkv, ("fsdp", "rep"), axis=0, tiled=True),
+        lax.all_gather(w_out, ("fsdp", "rep"), axis=0, tiled=True),
+        lax.all_gather(w_up, ("fsdp", "rep"), axis=0, tiled=True),
+        lax.all_gather(w_down, ("fsdp", "rep"), axis=0, tiled=True),
         lax.all_gather(gains, ("fsdp", "rep"), axis=1, tiled=True),
         lax.all_gather(shifts, ("fsdp", "rep"), axis=1, tiled=True),
         lax.all_gather(b_up, ("fsdp", "rep"), axis=0, tiled=True),
@@ -393,14 +680,12 @@
     )
 
 
-def fetch_backward(whole, w_qkv, w_out, w_up, w_down, gains, shifts):
-    if whole is None:
-        whole = [
-            lax.all_gather(w, ("fsdp", "rep"), axis=0, tiled=True)
-            for w in (w_qkv, w_out, w_up, w_down)
-        ]
+def fetch_backward(w_qkv, w_out, w_up, w_down, gains, shifts):
     return (
-        *whole,
+        lax.all_gather(w_qkv, ("fsdp", "rep"), axis=0, tiled=True),
+        lax.all_gather(w_out, ("fsdp", "rep"), axis=0, tiled=True),
+        lax.all_gather(w_up, ("fsdp", "rep"), axis=0, tiled=True),
+        lax.all_gather(w_down, ("fsdp", "rep"), axis=0, tiled=True),
         lax.all_gather(gains, ("fsdp", "rep"), axis=1, tiled=True),
         lax.all_gather(shifts, ("fsdp", "rep"), axis=1, tiled=True),
     )
@@ -458,22 +743,28 @@
 ):
     row_count = caption_lengths.shape[0]
     near = lax.axis_size("fsdp") == 16 and lax.axis_size("rep") == 2
-    weights = gather_all(qkv_weight, out_weight, up_weight, down_weight) if near else None
+    if near:
+        weights, short = gather_all(
+            qkv_weight, out_weight, up_weight, down_weight, pack_small(norm_gain, norm_bias, up_bias, down_bias)
+        )
+        short = unpack_small(short)
     captions = caption_ids(caption_lengths)
     hidden = hidden_in.astype(jnp.float32)
     stored = []
     for layer_number in range(LAYERS):
-        fetched = fetch_forward(
-            weights[layer_number] if near else None,
-            qkv_weight[layer_number],
-            out_weight[layer_number],
-            up_weight[layer_number],
-            down_weight[layer_number],
-            norm_gain[layer_number],
-            norm_bias[layer_number],
-            up_bias[layer_number],
-            down_bias[layer_number],
-        )
+        if near:
+            fetched = (*weights[layer_number], *short[layer_number])
+        else:
+            fetched = fetch_forward(
+                qkv_weight[layer_number],
+                out_weight[layer_number],
+                up_weight[layer_number],
+                down_weight[layer_number],
+                norm_gain[layer_number],
+                norm_bias[layer_number],
+                up_bias[layer_number],
+                down_bias[layer_number],
+            )
         w_qkv, w_out, w_up, w_down, gains, shifts, b_up, b_down = fetched
         gains_full = gains.astype(jnp.float32)
         shifts_full = shifts.astype(jnp.float32)
@@ -497,30 +788,33 @@
         hidden = output
     gradient = grad_out.astype(jnp.float32)
     settled = [None] * LAYERS
+    kept, sums = [None] * LAYERS, [None] * LAYERS
     for layer_number in reversed(range(LAYERS)):
         layer_in, packed, logsum, middle, normed_f, preact, active, weights_kept = stored[
             layer_number
         ]
-        fetched = fetch_backward(
-            weights[layer_number] if near else None,
-            qkv_weight[layer_number],
-            out_weight[layer_number],
-            up_weight[layer_number],
-            down_weight[layer_number],
-            norm_gain[layer_number],
-            norm_bias[layer_number],
-        )
+        if near:
+            fetched = (*weights[layer_number], *short[layer_number][:2])
+        else:
+            fetched = fetch_backward(
+                qkv_weight[layer_number],
+                out_weight[layer_number],
+                up_weight[layer_number],
+                down_weight[layer_number],
+                norm_gain[layer_number],
+                norm_bias[layer_number],
+            )
         w_qkv, w_out, w_up, w_down, gains, shifts = fetched
         gains_full = gains.astype(jnp.float32)
         shifts_full = shifts.astype(jnp.float32)
         grad_low = gradient.astype(jnp.bfloat16)
         d_bdown = jnp.sum(grad_low.astype(jnp.float32), axis=0)
-        d_down = transposed_left(active, grad_low)
+        d_down = None if near else transposed_left(active, grad_low)
         d_active = transposed_right(grad_low, w_down)
         gelu_value, gelu_back = jax.vjp(exact_gelu, preact)
         d_preact = gelu_back(d_active)[0].astype(jnp.bfloat16)
         d_bup = jnp.sum(d_preact.astype(jnp.float32), axis=0)
-        d_up = transposed_left(normed_f, d_preact)
+        d_up = None if near else transposed_left(normed_f, d_preact)
         d_normed_f = transposed_right(d_preact, w_up)
         norm_value, norm_back = jax.vjp(layer_norm, middle, gains_full[1], shifts_full[1])
         d_middle_ln, d_gain_f, d_shift_f = norm_back(d_normed_f)
@@ -539,6 +833,12 @@
         first_value, first_back = jax.vjp(layer_norm, layer_in, gains_full[0], shifts_full[0])
         d_input_ln, d_gain_a, d_shift_a = first_back(d_normed_a)
         gradient = d_middle + d_input_ln
+        if near:
+            kept[layer_number] = (active, grad_low, normed_f, d_preact)
+            sums[layer_number] = (
+                jnp.stack([d_gain_a, d_gain_f]), jnp.stack([d_shift_a, d_shift_f]), d_bup, d_bdown
+            )
+            continue
         settled[layer_number] = settle(
             d_up,
             d_down,
@@ -547,6 +847,10 @@
             d_bup,
             d_bdown,
         )
+    if near:
+        d_up_all, d_down_all, short = scatter_all(*[jnp.stack(v) for v in zip(*kept)], pack_sums(sums))
+        short = short.reshape(LAYERS, 8, 128)
+        return (hidden, gradient, short[:, 0:2, :24], short[:, 2:4, :24], d_up_all, short[:, 5, :96], d_down_all, short[:, 4, :24])
     d_gains = jnp.stack([settled[number][2] for number in range(LAYERS)])
     d_shifts = jnp.stack([settled[number][3] for number in range(LAYERS)])
     d_up_all = jnp.stack([settled[number][0] for number in range(LAYERS)])

time: 1240 us -> 505 us (0.41)
  waiting for transfers between devices: 543 us -> 0 us
  blocking collectives: 201 us -> 0 us
  Pallas kernels: 128 us -> 252 us
  local copies, waits for them, and re-layouts: 134 us -> 47.5 us
  matrix products: 168 us -> 141 us
  other arithmetic: 37.8 us -> 52.6 us
  between operations: 15.6 us -> 2.36 us
    unnamed x2 -> x0, waiting for transfers between devices: 543 us -> none
    all_gather x4 -> x0, blocking collectives: 158 us -> none  [the longest x2 83 us: fetch_forward(): lax.all_gather(shifts, ('fsdp', 'rep'), axis=1, tiled=True)]
    pallas_call x0 -> x1, Pallas kernels: none -> 119 us  [scatter_all(): pl.pallas_call(scatter_kernel, out_shape=[jax.ShapeDtypeStruct((2, 24, FF...]
    unnamed x1 -> x0, blocking collectives: 42.2 us -> none
    unnamed x193 -> x164, local copies, waits for them, and re-layouts: 53.7 us -> 16.3 us
    reshape x12 -> x1, local copies, waits for them, and re-layouts: 33.8 us -> 0.86 us  [pack_sums(): return both.reshape(ZS, YS, XS, 2, 16, 128).transpose(3, 0, 1, 2, 4, 5)]
    dot_general x4 -> x0, matrix products: 21.5 us -> none  [transposed_left(): lax.dot_general(left, right, (((0,), (0,)), ((), ())), preferred_element_...]
    another operation x6 -> x5, other arithmetic: 4.01 us -> 18.4 us  [per_device(): jnp.stack(v)]
  transfers between devices with their start and end apart: 1 -> 0, of which waited for: 1 -> 0; matrix products, arithmetic and copies ran while one was open for 1% -> 0% of each run, Pallas kernels for 0% -> 0%
where the time goes in v2:
time: 505 us; the launch traced here: 495 us
  Pallas kernels  252 us (50%)
  matrix products  141 us (28%)
  other arithmetic  52.6 us (10%)
  local copies, waits for them, and re-layouts  47.5 us (9%)
    pallas_call x1, Pallas kernels, gather_all(): pl.pallas_call(gather_kernel, out_shape=[jax.ShapeDtypeStruct(s, jnp.bflo...  132 us
    pallas_call x1, Pallas kernels, scatter_all(): pl.pallas_call(scatter_kernel, out_shape=[jax.ShapeDtypeStruct((2, 24, FF...  119 us
    dot_general x2, matrix products, per_device(): jnp.dot(normed_f, w_up, preferred_element_type=jnp.float32)  39.6 us
    dot_general x8, matrix products, transposed_right(): lax.dot_general(left, right, (((1,), (1,)), ((), ())), preferred_element_...  33.2 us
    another operation x5, other arithmetic, per_device(): jnp.stack(v)  18.4 us
    dot_general x2, matrix products, attend_back(): jnp.einsum('qhd,khd->hqk', d_heads, values_part, preferred_element_type=j...  17.4 us
    dot_general x2, matrix products, attend_back(): jnp.einsum('hqk,qhd->khd', probs.astype(jnp.bfloat16), d_heads, preferred...  17 us
    unnamed x164, local copies, waits for them, and re-layouts  16.3 us

profile of v2, /device:TPU:0, one launch (start us, length us, event | category | flops | bytes accessed | tf_op | source)
XLA Modules:
  0.0 495.0 jit_solution(4990137988958849953)
XLA Ops:
  14.9 132.2 %shard_map.170 = (bf16[4,2,2,48,2304]{4,3,2,1,0:T(8,128)(2,1)}, bf16[4,2,2,48,768]{4,3,2,1,0:T(8,128)(2,1)}, bf16[4,2,2,48,3072]{4,3,2,1,0:T(8,128)(2,1)}, bf16[...) custom-call(bf16[2,32,6144]{2,1,0:T(8,128)(2,1)} %pad.46.pin_ref, ...), custom_call_target="tpu_custom_call" | custom-call | tf_op jit(solution)/shard_map/pallas_call | solution.py:368
  151.7 4.1 convolution_convert_fusion.1
  159.2 2.1 fusion.31
  161.3 2.6 fusion
  165.8 3.8 fusion.63
  171.5 19.9 %multiply_convert_fusion.3 = (bf16[512,3072]{1,0:T(8,128)(2,1)S(1)}, f32[512,3072]{1,0:T(8,128)}, f32[512,3072]{1,0:T(8,128)}) fusion(f32[3072]{0:T(1024)S(1)} %reshape.491, bf16[768,3072]{1,0:T(8,128)(2,1)} %bitcast.215, f32[512,768]{1,0:T(8,128)S(1)} %get-tuple-element.155, f32[768]{0:T(1024)S(1)} %add.208, f32[768]{0:T(1024)S(1)} %mul.364, ...), kind=kOutput, calls=%fused_computation.51 | convolution fusion | flops 2521694208 | bytes 22042624 | tf_op jit(solution)/shard_map/dot_general | solution.py:777
  191.5 2.7 fusion.118
  194.6 2.2 convolution_convert_fusion
  199.8 2.3 copy.84
  202.1 2.1 fusion.32
  204.2 2.6 fusion.1
  208.7 5.0 %fusion.62 = bf16[12,64,512]{2,1,0:T(8,128)(2,1)S(1)} fusion(bf16[512,12,64]{0,2,1:T(8,128)(2,1)} %bitcast.186, f32[12,512]{1,0:T(8,128)S(1)} %fusion.1, f32[12,512]{1,0:T(8,128)S(1)} %get-tuple-element.159, f32[12,512,512]{1,2,0:T(8,128)S(1)} %get-tuple-element.160, pred[512,512]{0,1:T(8,128)(4,1)S(1)} %broadcast_compare_fusion), kind=kOutput, calls=%fused_computation.133 | convolution fusion | flops 418775040 | bytes 14467072 | tf_op jit(solution)/shard_map/while/body/eval_jaxpr/hqk,khd->qhd/dot_general | solution.py:75
  214.9 19.7 %multiply_convert_fusion.2 = (bf16[512,3072]{1,0:T(8,128)(2,1)S(1)}, f32[512,3072]{1,0:T(8,128)}, f32[512,3072]{1,0:T(8,128)}) fusion(f32[3072]{0:T(1024)S(1)} %reshape.493, bf16[768,3072]{1,0:T(8,128)(2,1)} %bitcast.223, f32[512,768]{1,0:T(8,128)S(1)} %get-tuple-element.162, f32[768]{0:T(1024)S(1)} %add.222, f32[768]{0:T(1024)S(1)} %mul.380, ...), kind=kOutput, calls=%fused_computation.38 | convolution fusion | flops 2521694208 | bytes 22042624 | tf_op jit(solution)/shard_map/dot_general | solution.py:777
  234.7 8.9 %convert_reduce_fusion = (f32[3072]{0:T(1024)S(1)}, bf16[512,3072]{1,0:T(8,128)(2,1)S(1)}) fusion(f32[512,3072]{1,0:T(8,128)} %get-tuple-element.122, bf16[3072,768]{1,0:T(8,128)(2,1)S(1)} %bitcast.229, bf16[512,768]{1,0:T(8,128)(2,1)S(1)} %copy-done.17, f32[512,3072]{1,0:T(8,128)} %get-tuple-element.163, f32[3072]{0:T(1024)S(1)} %reshape.493), kind=kOutput, calls=%fused_computation.33 | convolution fusion | flops 2442654720 | bytes 21258240 | tf_op jit(solution)/shard_map/dot_general | solution.py:46
  243.6 3.7 add_add_fusion.7
  247.3 3.0 multiply_reduce_fusion.2
  254.9 2.3 copy.89
  258.0 8.1 %fusion.56 = bf16[12,64,512]{2,1,0:T(8,128)(2,1)S(1)} fusion(bf16[512,12,64]{0,2,1:T(8,128)(2,1)} %bitcast.190, f32[12,512]{1,0:T(8,128)S(1)} %log_add_fusion.1, f32[12,512,512]{1,2,0:T(8,128)} %copy-done.1, pred[512,512]{0,1:T(8,128)(4,1)S(1)} %broadcast_compare_fusion), kind=kOutput, calls=%fused_computation.131 | convolution fusion | flops 415629312 | bytes 14442496 | tf_op jit(solution)/shard_map/while/body/eval_jaxpr/hqk,qhd->khd/dot_general | solution.py:84
  266.1 6.3 %pad_maximum_fusion.act_ref = bf16[2,512,3072]{2,1,0:T(8,128)(2,1)} fusion(bf16[1,512,3072]{2,1,0:T(8,128)(2,1)} %bitcast.195, bf16[1,512,3072]{2,1,0:T(8,128)(2,1)} %bitcast.194), kind=kLoop, calls=%fused_computation.22 | loop fusion | flops 3145728 | bytes 12582912 | tf_op jit(solution)/shard_map/stack | solution.py:851
  272.4 6.6 %multiply_reduce_fusion.1 = (f32[12,512]{1,0:T(8,128)S(1)}, f32[12,512,512]{1,2,0:T(8,128)}) fusion(f32[12,512]{1,0:T(8,128)S(1)} %log_add_fusion.1, f32[12,512,512]{1,2,0:T(8,128)S(1)} %bitcast.175, pred[512,512]{0,1:T(8,128)(4,1)S(1)} %broadcast_compare_fusion, bf16[512,12,64]{0,2,1:T(8,128)(2,1)S(1)} %bitcast.191, bf16[512,12,64]{0,2,1:T(8,128)(2,1)S(1)} %bitcast.187), kind=kOutput, calls=%fused_computation.4 | convolution fusion | flops 418375680 | bytes 27049984 | tf_op jit(solution)/shard_map/while/body/eval_jaxpr/qhd,khd->hqk/dot_general | solution.py:87
  279.0 7.4 %multiply_convert_fusion.1 = bf16[12,512,512]{1,2,0:T(8,128)(2,1)S(1)} fusion(f32[12,512,512]{1,2,0:T(8,128)} %get-tuple-element.166, f32[12,512]{1,0:T(8,128)S(1)} %get-tuple-element.165, f32[12,512]{1,0:T(8,128)S(1)} %log_add_fusion.1, f32[12,512,512]{1,2,0:T(8,128)S(1)} %bitcast.175, pred[512,512]{0,1:T(8,128)(4,1)S(1)} %broadcast_compare_fusion), kind=kLoop, calls=%fused_computation.3 | loop fusion | flops 18874368 | bytes 31768576 | tf_op jit(solution)/shard_map/while/body/eval_jaxpr/convert_element_type | solution.py:89
  290.5 3.0 multiply_reduce_fusion.3
  295.2 8.9 %convert_reduce_fusion.1 = (f32[3072]{0:T(1024)S(1)}, bf16[512,3072]{1,0:T(8,128)(2,1)S(1)}) fusion(f32[512,3072]{1,0:T(8,128)} %get-tuple-element.124, bf16[3072,768]{1,0:T(8,128)(2,1)} %bitcast.219, f32[512,768]{1,0:T(8,128)S(1)} %get-tuple-element.114, f32[512,3072]{1,0:T(8,128)} %get-tuple-element.156, f32[3072]{0:T(1024)S(1)} %copy-done.47), kind=kOutput, calls=%fused_computation.34 | convolution fusion | flops 2443047936 | bytes 22044672 | tf_op jit(solution)/shard_map/dot_general | solution.py:46
  304.2 3.5 multiply_reduce_fusion.4
  311.1 2.3 copy.93
  313.4 6.2 %pad_maximum_fusion.1.dp_ref = bf16[2,512,3072]{2,1,0:T(8,128)(2,1)} fusion(bf16[1,512,3072]{2,1,0:T(8,128)(2,1)} %bitcast.193, bf16[1,512,3072]{2,1,0:T(8,128)(2,1)} %bitcast.196), kind=kLoop, calls=%fused_computation.23 | loop fusion | flops 3145728 | bytes 12582912 | tf_op jit(solution)/shard_map/stack | solution.py:851
  325.4 9.0 %fusion.59 = bf16[12,64,512]{2,1,0:T(8,128)(2,1)} fusion(bf16[512,12,64]{0,2,1:T(8,128)(2,1)} %bitcast.188, f32[12,512]{1,0:T(8,128)S(1)} %copy-done.26, f32[12,512,512]{1,2,0:T(8,128)} %copy-done, pred[512,512]{0,1:T(8,128)(4,1)S(1)} %broadcast_compare_fusion), kind=kOutput, calls=%fused_computation.132 | convolution fusion | flops 415629312 | bytes 14442496 | tf_op jit(solution)/shard_map/while/body/eval_jaxpr/hqk,qhd->khd/dot_general | solution.py:84
  335.7 10.8 %multiply_reduce_fusion = (f32[12,512]{1,0:T(8,128)S(1)}, f32[12,512,512]{1,2,0:T(8,128)}) fusion(f32[12,512]{1,0:T(8,128)S(1)} %copy-done.26, f32[12,512,512]{1,2,0:T(8,128)} %copy-done, pred[512,512]{0,1:T(8,128)(4,1)S(1)} %broadcast_compare_fusion, bf16[512,12,64]{0,2,1:T(8,128)(2,1)S(1)} %bitcast.189, bf16[512,12,64]{0,2,1:T(8,128)(2,1)S(1)} %bitcast.185), kind=kOutput, calls=%fused_computation.1 | convolution fusion | flops 418375680 | bytes 27049984 | tf_op jit(solution)/shard_map/while/body/eval_jaxpr/qhd,khd->hqk/dot_general | solution.py:87
  346.5 7.3 %multiply_convert_fusion = bf16[12,512,512]{1,2,0:T(8,128)(2,1)S(1)} fusion(f32[12,512,512]{1,2,0:T(8,128)} %get-tuple-element.170, f32[12,512]{1,0:T(8,128)S(1)} %get-tuple-element.169, f32[12,512]{1,0:T(8,128)S(1)} %copy-done.26, f32[12,512,512]{1,2,0:T(8,128)S(1)} %bitcast.173, pred[512,512]{0,1:T(8,128)(4,1)S(1)} %broadcast_compare_fusion), kind=kLoop, calls=%fused_computation | loop fusion | flops 18874368 | bytes 31768576 | tf_op jit(solution)/shard_map/while/body/eval_jaxpr/convert_element_type | solution.py:89
  358.3 2.3 fusion.102
  364.8 2.7 pad_maximum_fusion.2.g_ref
  367.5 119.4 %shard_map.171 = (f32[2,24,3072]{2,1,0:T(8,128)}, f32[2,96,768]{2,1,0:T(8,128)}, f32[16,128]{1,0:T(8,128)}) custom-call(bf16[2,512,3072]{2,1,0:T(8,128)(2,1)} %pad_maximum_fusion.act_ref, bf16[2,512,768]{2,1,0:T(8,128)(2,1)} %pad_maximum_fusion.2.g_ref, bf16[2,512,768]{2,1,0:T(8,128)(2,1)} %pad_maximum_fusion.3.nf_ref, ...), custom_call_target="tpu_custom_call" | custom-call | tf_op jit(solution)/shard_map/pallas_call | solution.py:633
  (271 shorter events, 70.1 us)
Async XLA Ops:
  0.6 151.0 %copy-start.2 = (bf16[512,768]{1,0:T(8,128)(2,1)S(1)}, bf16[512,768]{1,0:T(8,128)(2,1)}, u32[]{:S(2)}) copy-start(bf16[512,768]{1,0:T(8,128)(2,1)} %param.11) | copy-start | bytes 2359300
  7.0 148.9 %copy-start.32 = (f32[512]{0:T(512)}, f32[512]{0:T(512)S(1)}, u32[]{:S(2)}) copy-start(f32[512]{0:T(512)S(1)} %broadcast_multiply_fusion.3) | copy-start | bytes 6148
  8.5 138.6 %copy-start.38 = (f32[512]{0:T(512)}, f32[512]{0:T(512)S(1)}, u32[]{:S(2)}) copy-start(f32[512]{0:T(512)S(1)} %fusion.54) | copy-start | bytes 6148
  8.5 147.4 %copy-start.34 = (f32[512]{0:T(512)}, f32[512]{0:T(512)S(1)}, u32[]{:S(2)}) copy-start(f32[512]{0:T(512)S(1)} %fusion.79) | copy-start | bytes 6148
  148.2 23.3 %copy-start.46 = (f32[3072]{0:T(1024)}, f32[3072]{0:T(1024)S(1)}, u32[]{:S(2)}) copy-start(f32[3072]{0:T(1024)S(1)} %reshape.491) | copy-start | bytes 36868
  151.4 20.1 %copy-start.42 = (f32[768]{0:T(1024)}, f32[768]{0:T(1024)S(1)}, u32[]{:S(2)}) copy-start(f32[768]{0:T(1024)S(1)} %add.208) | copy-start | bytes 9220
  151.6 19.9 %copy-start.44 = (f32[768]{0:T(1024)}, f32[768]{0:T(1024)S(1)}, u32[]{:S(2)}) copy-start(f32[768]{0:T(1024)S(1)} %mul.364) | copy-start | bytes 9220
  169.7 21.9 %slice-start.8 = ((s8[4718592]{0:T(1024)(128)(4,1)}), s8[4194304]{0:T(1024)(128)(4,1)S(1)}, s32[]{:S(2)}) async-start(s8[4718592]{0:T(1024)(128)(4,1)} %bitcast.220), calls=%async_computation.8 | async-start | bytes 8388608
  170.6 20.9 %copy-start.8 = (f32[512,768]{1,0:T(8,128)}, f32[512,768]{1,0:T(8,128)S(1)}, u32[]{:S(2)}) copy-start(f32[512,768]{1,0:T(8,128)S(1)} %get-tuple-element.155) | copy-start | bytes 4718596
  170.6 20.9 %copy-start.36 = (f32[512]{0:T(512)}, f32[512]{0:T(512)S(1)}, u32[]{:S(2)}) copy-start(f32[512]{0:T(512)S(1)} %broadcast_multiply_fusion.2) | copy-start | bytes 6148
  171.5 20.0 %copy-start.48 = (f32[512]{0:T(512)}, f32[512]{0:T(512)S(1)}, u32[]{:S(2)}) copy-start(f32[512]{0:T(512)S(1)} %fusion.80) | copy-start | bytes 6148
  171.5 20.0 %slice-start.9 = ((s8[4718592]{0:T(1024)(128)(4,1)}), s8[524288]{0:T(1024)(128)(4,1)S(1)}, s32[]{:S(2)}) async-start(s8[4718592]{0:T(1024)(128)(4,1)} %bitcast.220), calls=%async_computation.9 | async-start | bytes 1048576
  213.7 21.0 %slice-start.12 = ((s8[4718592]{0:T(1024)(128)(4,1)}), s8[4194304]{0:T(1024)(128)(4,1)S(1)}, s32[]{:S(2)}) async-start(s8[4718592]{0:T(1024)(128)(4,1)} %bitcast.227), calls=%async_computation.12 | async-start | bytes 8388608
  213.7 33.7 %slice-start.10 = ((s8[4718592]{0:T(1024)(128)(4,1)}), s8[524288]{0:T(1024)(128)(4,1)S(1)}, s32[]{:S(2)}) async-start(s8[4718592]{0:T(1024)(128)(4,1)} %bitcast.224), calls=%async_computation.10 | async-start | bytes 1048576
  214.9 19.7 %copy-start.17 = (bf16[512,768]{1,0:T(8,128)(2,1)S(1)}, bf16[512,768]{1,0:T(8,128)(2,1)}, u32[]{:S(2)}) copy-start(bf16[512,768]{1,0:T(8,128)(2,1)} %param.21) | copy-start | bytes 2359300
  214.9 19.7 %slice-start.13 = ((s8[4718592]{0:T(1024)(128)(4,1)}), s8[524288]{0:T(1024)(128)(4,1)S(1)}, s32[]{:S(2)}) async-start(s8[4718592]{0:T(1024)(128)(4,1)} %bitcast.227), calls=%async_computation.13 | async-start | bytes 1048576
  214.9 32.4 %slice-start.11 = ((s8[4718592]{0:T(1024)(128)(4,1)}), s8[4194304]{0:T(1024)(128)(4,1)S(1)}, s32[]{:S(2)}) async-start(s8[4718592]{0:T(1024)(128)(4,1)} %bitcast.224), calls=%async_computation.11 | async-start | bytes 8388608
  258.0 14.4 %slice-start.3 = ((s8[12582912]{0:T(1024)(128)(4,1)}), s8[4194304]{0:T(1024)(128)(4,1)S(1)}, s32[]{:S(2)}) async-start(s8[12582912]{0:T(1024)(128)(4,1)} %bitcast.174), calls=%async_computation.3 | async-start | bytes 8388608
  258.0 14.4 %slice-start.4 = ((s8[12582912]{0:T(1024)(128)(4,1)}), s8[4194304]{0:T(1024)(128)(4,1)S(1)}, s32[]{:S(2)}) async-start(s8[12582912]{0:T(1024)(128)(4,1)} %bitcast.174), calls=%async_computation.4 | async-start | bytes 8388608
  294.2 10.0 %slice-start.6 = ((s8[4718592]{0:T(1024)(128)(4,1)}), s8[4194304]{0:T(1024)(128)(4,1)S(1)}, s32[]{:S(2)}) async-start(s8[4718592]{0:T(1024)(128)(4,1)} %bitcast.216), calls=%async_computation.6 | async-start | bytes 8388608
  295.2 9.0 %copy-start.45 = (f32[768]{0:T(1024)S(1)}, f32[768]{0:T(1024)}, u32[]{:S(2)}) copy-start(f32[768]{0:T(1024)} %copy-done.44) | copy-start | bytes 9220
  295.2 9.0 %copy-start.49 = (f32[512]{0:T(512)S(1)}, f32[512]{0:T(512)}, u32[]{:S(2)}) copy-start(f32[512]{0:T(512)} %copy-done.48) | copy-start | bytes 6148
  295.2 9.0 %slice-start.7 = ((s8[4718592]{0:T(1024)(128)(4,1)}), s8[524288]{0:T(1024)(128)(4,1)S(1)}, s32[]{:S(2)}) async-start(s8[4718592]{0:T(1024)(128)(4,1)} %bitcast.216), calls=%async_computation.7 | async-start | bytes 1048576
  309.3 10.3 %copy-start.50 = (f32[512]{0:T(512)}, f32[512]{0:T(512)S(1)}, u32[]{:S(2)}) copy-start(f32[512]{0:T(512)S(1)} %negate_multiply_fusion.3) | copy-start | bytes 6148
  313.4 11.9 %copy-start.26 = (f32[12,512]{1,0:T(8,128)S(1)}, f32[12,512]{1,0:T(8,128)}, u32[]{:S(2)}) copy-start(f32[12,512]{1,0:T(8,128)} %log_add_fusion) | copy-start | bytes 73732
  325.4 9.0 %copy-start.23 = (bf16[1,512,768]{2,1,0:T(8,128)(2,1)S(1)}, bf16[1,512,768]{2,1,0:T(8,128)(2,1)}, u32[]{:S(2)}) copy-start(bf16[1,512,768]{2,1,0:T(8,128)(2,1)} %get-tuple-element.132) | copy-start | bytes 2359300
  325.4 9.0 %copy-start.24 = (bf16[1,512,768]{2,1,0:T(8,128)(2,1)S(1)}, bf16[1,512,768]{2,1,0:T(8,128)(2,1)}, u32[]{:S(2)}) copy-start(bf16[1,512,768]{2,1,0:T(8,128)(2,1)} %get-tuple-element.131) | copy-start | bytes 2359300
  325.4 10.3 %copy-start.13 = (bf16[512,768]{0,1:T(8,128)(2,1)S(1)}, bf16[512,768]{0,1:T(8,128)(2,1)}, u32[]{:S(2)}) copy-start(bf16[512,768]{0,1:T(8,128)(2,1)} %copy-done.12) | copy-start | bytes 2359300
  325.4 10.3 %copy-start.15 = (bf16[512,768]{0,1:T(8,128)(2,1)S(1)}, bf16[512,768]{0,1:T(8,128)(2,1)}, u32[]{:S(2)}) copy-start(bf16[512,768]{0,1:T(8,128)(2,1)} %copy.93) | copy-start | bytes 2359300
  334.4 12.1 %slice-start = ((s8[12582912]{0:T(1024)(128)(4,1)}), s8[4194304]{0:T(1024)(128)(4,1)S(1)}, s32[]{:S(2)}) async-start(s8[12582912]{0:T(1024)(128)(4,1)} %bitcast.172), calls=%async_computation | async-start | bytes 8388608
  335.6 10.8 %slice-start.1 = ((s8[12582912]{0:T(1024)(128)(4,1)}), s8[4194304]{0:T(1024)(128)(4,1)S(1)}, s32[]{:S(2)}) async-start(s8[12582912]{0:T(1024)(128)(4,1)} %bitcast.172), calls=%async_computation.1 | async-start | bytes 8388608
  335.6 10.9 %slice-start.2 = ((s8[12582912]{0:T(1024)(128)(4,1)}), s8[4194304]{0:T(1024)(128)(4,1)S(1)}, s32[]{:S(2)}) async-start(s8[12582912]{0:T(1024)(128)(4,1)} %bitcast.172), calls=%async_computation.2 | async-start | bytes 8388608
  (41 other events, 163.7 us)
